TPU v7x, 32 devices: a whole 2x2x4 slice. The times are simulated.
32 devices in a mesh: comp: 2 (over core), lat: 4 (over z), lon: 4 (over y, x).
Axes of the slice: x: 2, y: 2, z: 4, core: 2. Of those that a mesh axis runs over, the one named last changes fastest.
Arguments:
- state_field: bfloat16 [2, 128, 128, 768], P('comp', 'lat', 'lon'), may hold values from -8 to 8
- sea_mask: int32 [128, 128], P('lat', 'lon'), may hold values from 0 to 1, as said below
- w_qkv: bfloat16 [768, 2304], replicated, may hold values from -1 to 1
- w_attn_out: bfloat16 [768, 768], replicated, may hold values from -0.21875 to 0.21875
- w_up: bfloat16 [768, 3072], replicated, may hold values from -0.21875 to 0.21875
- w_down: bfloat16 [3072, 768], replicated, may hold values from -0.109375 to 0.109375
- conv_weight: bfloat16 [4, 3, 3, 128, 128], replicated, may hold values from -0.1875 to 0.1875
- conv_bias: float32 [4, 128], replicated, may hold values from -3 to 3
- w_surface: bfloat16 [2, 768, 256], P('comp'), may hold values from -0.21875 to 0.21875
- w_forcing: bfloat16 [2, 256, 768], P('comp'), may hold values from -0.375 to 0.375
- regrid_blocks: bfloat16 [2, 4, 256, 256], replicated, may hold values from -0.375 to 0.375
- routes: int32 [2, 4, 4, 1024, 2], P('comp', 'lat', 'lon'), may hold values from 0 to 15, all different within a row; in each aligned block of 1024 rows (0 to 1023, 1024 to 2047, ..., all dimensions but the last counted through in order) at most 192 rows name the same one
- dest_entry: int32 [2, 4, 4, 1024, 2], P('comp', 'lat', 'lon'), may hold values from 0 to 1023
- block_index: int32 [2, 4, 4, 1024, 2], P('comp', 'lat', 'lon'), may hold values from 0 to 3
Outputs:
- new_field: bfloat16 [2, 128, 128, 768], P('comp', 'lat', 'lon')
Inputs may be any that keep to these rules, and one draw needn't show every extreme that they name: `sea_mask`: 1 marks sea and 0 land; the share of land is drawn anew for each band of 32 rows. routes[c, i, j, e, t] numbers the device of component 1 - c that link t of entry e of device (i, j) feeds; the 2 links of an entry name different devices; the entries of one device name one destination at most 192 times, a bound that some block reaches. `dest_entry`: the destination entry, row-major within the destination device's block. `block_index`: the sending component's regridding block that the link applies.
All inputs are finite; a program needn't handle non-finite values.
Results may differ from a plain program's by a relative error of at most 0.007.
Values may be sent and summed in bfloat16 or wider, within the bound.
A program may use at most 192 MiB of HBM per device.

v0:
```python
import functools

import jax
import jax.numpy as jnp
from jax import lax
from jax.experimental import pallas as pl
from jax.experimental.pallas import tpu as pltpu
from jax.sharding import PartitionSpec as P

HEAD = 64
OCH = 128
PACK = 6
WIN = 8
MARGIN = WIN // 2
EPSILON = 1e-05
RADIX = 32
COLPAD = 48
LABEL_ROWS = 16
VMEM_LIMIT = 56 * 1024 * 1024
F32 = jnp.float32
BF16 = jnp.bfloat16
VMEM = pltpu.VMEM
NT = (((1,), (1,)), ((), ()))


def normalize(values):
    average = jnp.mean(values, axis=-1, keepdims=True)
    centred = values - average
    spread = jnp.mean(centred * centred, axis=-1, keepdims=True)
    return centred * lax.rsqrt(spread + EPSILON)


def gelu(x):
    return 0.5 * x * (1.0 + jnp.tanh(0.7978845608028654 * (x + 0.044715 * (x * x * x))))


def iota(shape, dim):
    return lax.broadcasted_iota(jnp.int32, shape, dim)


def onehot(mask):
    return jnp.where(mask, 1.0, 0.0).astype(BF16)


def pack_kernel(surf_ref, table_ref, kind_ref, where_ref, out_ref, links_ref):
    groups, padded_cap, feat = out_ref.shape
    cap = padded_cap - LABEL_ROWS
    entries = surf_ref.shape[0]
    routes = [where_ref[t : t + 1, :] for t in range(2)]
    device = iota((groups, entries), 0)
    match = [jnp.where(device == route, 1.0, 0.0) for route in routes]
    earlier = onehot(iota((entries, entries), 0) < iota((entries, entries), 1))
    counts = jnp.dot((match[0] + match[1]).astype(BF16), earlier, preferred_element_type=F32)
    position, label = [], []
    for t in range(2):
        slot = jnp.sum(match[t] * counts, axis=0, keepdims=True).astype(jnp.int32)
        position.append(routes[t] * cap + slot)
        value = where_ref[2 + t : 3 + t, :] + 1
        high = (value // RADIX).astype(F32)
        low = (value % RADIX).astype(F32)
        row = iota((LABEL_ROWS, entries), 0)
        label.append(jnp.where(row == 0, high, jnp.where(row == 1, low, 0.0)).astype(BF16))
    surf = surf_ref[...]
    spread = [
        jnp.dot(surf, table_ref[b], preferred_element_type=F32) for b in range(table_ref.shape[0])
    ]
    for t in range(2):
        kind = kind_ref[:, t : t + 1]
        total = jnp.where(kind == 0, spread[0], 0.0)
        for b in range(1, len(spread)):
            total = jnp.where(kind == b, spread[b], total)
        links_ref[t * entries : (t + 1) * entries, :] = total.astype(BF16)

    def body(g, carry):
        spot = iota((cap, entries), 0) + g * cap
        pick = jnp.concatenate([onehot(spot == position[t]) for t in range(2)], axis=1)
        rows = jnp.dot(pick, links_ref[...], preferred_element_type=F32)
        out_ref[g, 0:cap, :] = rows.astype(BF16)
        labels = lax.dot_general(
            jnp.concatenate(label, axis=1), pick, NT, preferred_element_type=F32
        ).astype(BF16)
        out_ref[g, cap:padded_cap, :] = jnp.zeros((LABEL_ROWS, feat), BF16)
        out_ref[g, cap:padded_cap, 0:cap] = labels
        return carry

    lax.fori_loop(0, groups, body, 0)


def finish_kernel(got_ref, core_ref, wf_ref, sea_ref, out_ref):
    groups, padded_cap, feat = got_ref.shape
    cap = padded_cap - LABEL_ROWS
    entries = core_ref.shape[0]
    step = 256
    labels = []
    for g in range(groups):
        both = got_ref[g, cap:padded_cap, 0:cap].astype(F32)
        labels.append((both[0:1] * RADIX + both[1:2] - 1.0).astype(jnp.int32))

    for i in range(entries // step):
        entry = iota((step, cap), 0) + i * step
        total = jnp.zeros((step, feat), F32)
        for g in range(groups):
            total = total + jnp.dot(
                onehot(entry == labels[g]), got_ref[g, 0:cap, :], preferred_element_type=F32
            )
        inject = jnp.dot(total.astype(BF16), wf_ref[...], preferred_element_type=F32)
        rows = slice(i * step, (i + 1) * step)
        out_ref[rows, :] = ((core_ref[rows, :] + inject) * sea_ref[rows, :]).astype(BF16)


def conv_kernel(place_ref, x_ref, w_ref, b_ref, out_ref, even_ref, odd_ref):
    ext_rows, cols, width = x_ref.shape
    layers = w_ref.shape[0]
    height, breadth, _ = out_ref.shape
    first_row, grid_rows = place_ref[0], place_ref[1]
    pairs = PACK // 2

    def put(dst, row, first, last):
        left = pltpu.roll(last.astype(F32), 1, 0).astype(BF16)
        right = pltpu.roll(first.astype(F32), cols - 1, 0).astype(BF16)
        dst[row, :, 0:OCH] = left
        dst[row, :, OCH + width :] = right

    def fill(r, carry):
        row = x_ref[r]
        even_ref[r, :, OCH : OCH + width] = row
        put(even_ref, r, row[:, 0:OCH], row[:, width - OCH :])
        return carry

    lax.fori_loop(MARGIN - layers, ext_rows - MARGIN + layers, fill, 0)
    block = 2
    for layer in range(layers):
        src, dst = (even_ref, odd_ref) if layer % 2 == 0 else (odd_ref, even_ref)
        start = MARGIN - layers + layer + 1
        steps = (ext_rows - 2 * start) // block
        bias = b_ref[layer : layer + 1, :]

        def body(i, carry, layer=layer, src=src, dst=dst, start=start, bias=bias):
            base = start + i * block
            parts = []
            for dy in range(3):
                rows = src[pl.ds(base - 1 + dy, block)].reshape(block * cols, -1)
                parts.append(
                    jnp.concatenate(
                        [rows[:, 256 * j : 256 * j + 512] for j in range(pairs)], axis=0
                    )
                )
            total = jnp.dot(
                jnp.concatenate(parts, axis=1), w_ref[layer], preferred_element_type=F32
            )
            active = gelu(total + bias)
            for k in range(block):
                row = base + k
                at = first_row + row
                inside = (at >= 0) & (at < grid_rows)
                cells = []
                for j in range(pairs):
                    begin = (j * block + k) * cols
                    lanes = slice(OCH + 256 * j, OCH + 256 * j + 256)
                    old = src[row, :, lanes].astype(F32)
                    new = jnp.where(inside, old + active[begin : begin + cols], 0.0)
                    cells.append(new.astype(BF16))
                    if layer < layers - 1:
                        dst[row, :, lanes] = cells[-1]
                    else:
                        out_ref[row - MARGIN, :, 256 * j : 256 * j + 256] = (
                            cells[-1][0:breadth].astype(F32)
                        )
                if layer < layers - 1:
                    put(dst, row, cells[0][:, 0:OCH], cells[-1][:, OCH:])
            return carry

        lax.fori_loop(0, steps, body, 0)


def attend_kernel(
    place_ref, x_ref, own_ref, wqkv_ref, wo_ref, wu_ref, wd_ref, out_ref,
    normed_ref, qkv_ref, wide_ref, att_ref,
):
    ext_rows, ext_cols, width = x_ref.shape
    win_rows, win_cols = ext_rows // WIN, ext_cols // WIN
    size = WIN * WIN
    height, breadth = ext_rows - 2 * MARGIN, ext_cols - 2 * MARGIN
    first_row, grid_rows = place_ref[0], place_ref[1]
    heads = 4
    lanes = heads * HEAD
    lane_head = iota((size, lanes), 1) // HEAD
    ones = onehot(iota((lanes, lanes), 0) // HEAD == iota((lanes, lanes), 1) // HEAD)

    def window_row(wr, carry):
        for wc in range(win_cols):
            tokens = jnp.concatenate(
                [
                    x_ref[wr * WIN + r, wc * WIN : (wc + 1) * WIN, :].astype(F32)
                    for r in range(WIN)
                ],
                axis=0,
            )
            normed_ref[wc * size : (wc + 1) * size, :] = normalize(tokens).astype(BF16)
        part = width
        for c in range(3):
            qkv = jnp.dot(
                normed_ref[...], wqkv_ref[:, c * part : (c + 1) * part], preferred_element_type=F32
            )
            if c == 0:
                qkv = qkv * HEAD ** (-0.5)
            qkv_ref[:, c * part : (c + 1) * part] = qkv.astype(BF16)
        key_row = first_row + wr * WIN + (iota((1, lanes), 1) % HEAD) // WIN
        key_ok = (key_row >= 0) & (key_row < grid_rows)

        def window(wc, carry):
            rows = pl.ds(wc * size, size)
            for group in range(width // lanes):
                at = group * lanes
                q = qkv_ref[rows, at : at + lanes]
                k = qkv_ref[rows, width + at : width + at + lanes]
                v = qkv_ref[rows, 2 * width + at : 2 * width + at + lanes]
                zero = jnp.zeros_like(k)
                ks = jnp.concatenate(
                    [jnp.where(lane_head == h, k, zero) for h in range(heads)], axis=0
                )
                vs = jnp.concatenate(
                    [jnp.where(lane_head == h, v, zero) for h in range(heads)], axis=0
                )
                scores = lax.dot_general(q, ks, NT, preferred_element_type=F32)
                scores = jnp.where(key_ok, scores, -1e30)
                halves = []
                for c in range(heads // 2):
                    s = scores[:, c * 128 : (c + 1) * 128]
                    low = lane_head[:, 0:128] == 0
                    m0 = jnp.max(jnp.where(low, s, -1e30), axis=1, keepdims=True)
                    m1 = jnp.max(jnp.where(low, -1e30, s), axis=1, keepdims=True)
                    halves.append(jnp.exp(s - jnp.where(low, m0, m1)))
                e = jnp.concatenate(halves, axis=1).astype(BF16)
                sums = jnp.dot(e, ones, preferred_element_type=F32)
                got = jnp.dot(e, vs, preferred_element_type=F32) / sums
                for r in range(WIN):
                    wide_ref[
                        wr * WIN + r, pl.ds(pl.multiple_of(wc * WIN, WIN), WIN), at : at + lanes
                    ] = got[r * WIN : (r + 1) * WIN]
            return carry

        lax.fori_loop(0, win_cols, window, 0)
        return carry

    lax.fori_loop(0, win_rows, window_row, 0)

    def gather(r, carry):
        att_ref[pl.ds(pl.multiple_of(r * breadth, breadth), breadth), :] = wide_ref[
            r + MARGIN, MARGIN : MARGIN + breadth, :
        ].astype(BF16)
        return carry

    lax.fori_loop(0, height, gather, 0)
    step = 256
    hid = wu_ref.shape[1]
    chunk = 768

    def mlp(i, carry):
        rows = pl.ds(pl.multiple_of(i * step, step), step)
        projected = jnp.dot(att_ref[rows, :], wo_ref[...], preferred_element_type=F32)
        first = (own_ref[rows, :].astype(F32) + projected).astype(BF16).astype(F32)
        second = normalize(first).astype(BF16)
        total = first
        for c in range(hid // chunk):
            cut = slice(c * chunk, (c + 1) * chunk)
            hidden = gelu(jnp.dot(second, wu_ref[:, cut], preferred_element_type=F32)).astype(BF16)
            total = total + jnp.dot(hidden, wd_ref[cut, :], preferred_element_type=F32)
        out_ref[rows, :] = total
        return carry

    lax.fori_loop(0, height * breadth // step, mlp, 0)


def call(kernel, shape, dtype, args, scratch, flops, smem_first=False):
    specs = [pl.BlockSpec(memory_space=VMEM) for _ in args]
    if smem_first:
        specs[0] = pl.BlockSpec(memory_space=pltpu.SMEM)
    return pl.pallas_call(
        kernel,
        out_shape=jax.ShapeDtypeStruct(shape, dtype),
        in_specs=specs,
        out_specs=pl.BlockSpec(memory_space=VMEM),
        scratch_shapes=scratch,
        compiler_params=pltpu.CompilerParams(vmem_limit_bytes=VMEM_LIMIT),
        cost_estimate=pl.CostEstimate(flops=flops, bytes_accessed=8 << 20, transcendentals=0),
    )(*args)


def pair_weights(conv_weight):
    layers = conv_weight.shape[0]
    zero = jnp.zeros_like(conv_weight[:, :, 0])
    w = [conv_weight[:, :, dx] for dx in range(3)]
    left = jnp.concatenate([w[0], w[1], w[2], zero], axis=2)
    right = jnp.concatenate([zero, w[0], w[1], w[2]], axis=2)
    return jnp.concatenate([left, right], axis=3).reshape(layers, 3 * 4 * OCH, 2 * OCH)


def convolve(extended, place, conv_weight, conv_bias):
    ext_rows, ext_cols, width = extended.shape
    height, breadth = ext_rows - 2 * MARGIN, ext_cols - 2 * MARGIN
    x = jnp.concatenate(
        [
            extended[:, MARGIN:],
            jnp.zeros((ext_rows, COLPAD - ext_cols, width), BF16),
            extended[:, :MARGIN],
        ],
        axis=1,
    )
    bias = jnp.concatenate([conv_bias, conv_bias], axis=1)
    scratch = [VMEM((ext_rows, COLPAD, width + 2 * OCH), BF16)] * 2
    core = call(
        conv_kernel, (height, breadth, width), F32,
        (place, x, pair_weights(conv_weight), bias), scratch, 40 * 10**9, True,
    )
    return core.reshape(height * breadth, width)


def attend(extended, own, place, w_qkv, w_attn_out, w_up, w_down):
    ext_rows, ext_cols, width = extended.shape
    entries = own.shape[0]
    scratch = [
        VMEM((ext_cols * WIN, width), BF16),
        VMEM((ext_cols * WIN, 3 * width), BF16),
        VMEM((ext_rows, ext_cols, width), F32),
        VMEM((entries, width), BF16),
    ]
    return call(
        attend_kernel, (entries, width), F32,
        (place, extended, own, w_qkv, w_attn_out, w_up, w_down), scratch, 60 * 10**9, True,
    )


def pack(surface, table, kind, where, groups, capacity):
    entries, feat = surface.shape
    return call(
        pack_kernel, (groups, capacity + LABEL_ROWS, feat), BF16, (surface, table, kind, where),
        [VMEM((2 * entries, feat), BF16)], 6 * 10**9,
    )


def finish(got, core, w_forcing, sea):
    return call(finish_kernel, core.shape, BF16, (got, core, w_forcing, sea), [], 6 * 10**9)


def padded(x, axis, dim, width, wrap):
    peers, length = (lax.axis_size(axis), x.shape[dim])
    up = [(i, (i + 1) % peers) for i in range(peers if wrap else peers - 1)]
    down = [(j, i) for i, j in up]
    last = lax.slice_in_dim(x, length - width, length, axis=dim)
    first = lax.slice_in_dim(x, 0, width, axis=dim)
    before = lax.ppermute(last, axis, up)
    after = lax.ppermute(first, axis, down)
    return jnp.concatenate([before, x, after], axis=dim)


def local(
    state_field, sea_mask, w_qkv, w_attn_out, w_up, w_down, conv_weight, conv_bias,
    w_surface, w_forcing, regrid_blocks, routes, dest_entry, block_index,
):
    component = lax.axis_index("comp")
    is_ocean = component == 1
    local_state = state_field[0]
    height, breadth, width = local_state.shape
    entries = height * breadth
    groups = lax.axis_size("lat") * lax.axis_size("lon")
    top = routes.shape[-1]
    capacity = 3 * entries * top // (2 * groups)
    sea = jnp.where(is_ocean, sea_mask, 1)
    initial = local_state * sea.astype(BF16)[:, :, None]
    swap = [(0, 1), (1, 0)]
    where = jnp.concatenate(
        [routes.reshape(entries, top).T, dest_entry.reshape(entries, top).T], axis=0
    )
    where = lax.ppermute(where, "comp", swap)
    kind = lax.ppermute(block_index.reshape(entries, top), "comp", swap)
    own = initial.reshape(entries, width)
    surface = jnp.dot(own, w_surface[0], preferred_element_type=F32).astype(BF16)
    surface = lax.ppermute(surface, "comp", swap)
    lon_wide = padded(initial, "lon", 1, MARGIN, True)
    extended = padded(lon_wide, "lat", 0, MARGIN, False)
    table = lax.dynamic_index_in_dim(regrid_blocks, 1 - component, 0, keepdims=False)
    outgoing = pack(surface, table, kind, where, groups, capacity)
    got = lax.all_to_all(outgoing, ("lat", "lon"), split_axis=0, concat_axis=0, tiled=True)
    first_row = lax.axis_index("lat") * height - MARGIN
    grid_rows = height * lax.axis_size("lat")
    place = jnp.stack([first_row, jnp.full_like(first_row, grid_rows)]).astype(jnp.int32)
    core = lax.cond(
        is_ocean,
        lambda ext: convolve(ext, place, conv_weight, conv_bias),
        lambda ext: attend(ext, own, place, w_qkv, w_attn_out, w_up, w_down),
        extended,
    )
    result = finish(got, core, w_forcing[0], sea.astype(F32).reshape(entries, 1))
    return result.reshape(1, height, breadth, width)


def solution(mesh):
    placed = (
        P("comp", "lat", "lon", None), P("lat", "lon"), P(), P(), P(), P(), P(), P(),
        P("comp", None, None), P("comp", None, None), P(),
        P("comp", "lat", "lon", None, None),
        P("comp", "lat", "lon", None, None),
        P("comp", "lat", "lon", None, None),
    )
    return jax.shard_map(
        local, mesh=mesh, in_specs=placed, out_specs=P("comp", "lat", "lon", None), check_vma=False
    )
```

profile of v0, /device:TPU:12, one launch (start us, length us, event | category | flops | bytes accessed | tf_op | source)
XLA Modules:
  0.0 131.5 jit_solution(12193343814190509543)
XLA Ops:
  0.0 0.0 copy-start
  0.0 0.0 copy-start.9
  0.0 0.0 copy-start.3
  0.0 0.0 copy-start.4
  0.1 0.0 copy-start.5
  0.1 1.7 %broadcast_multiply_fusion = bf16[1,32,32,768]{3,2,1,0:T(8,128)(2,1)S(1)} fusion(bf16[1,32,32,768]{3,2,1,0:T(8,128)(2,1)} %param.16, bf16[32,32]{1,0:T(8,128)(2,1)S(1)} %get-tuple-element.76), kind=kLoop, calls=%fused_computation.10 | loop fusion | flops 786432 | bytes 3147776 | tf_op jit(solution)/shard_map/mul | solution.py:370
  1.8 0.0 copy-done.9
  1.8 0.6 convolution_convert_fusion
  2.4 0.6 collective-permute-start
  3.0 0.0 copy-done.3
  3.0 0.2 copy.23
  3.2 0.1 collective-permute-start.1
  3.3 0.0 copy-done.4
  3.3 0.0 copy-done.5
  3.3 0.5 collective-permute-start.2
  3.9 0.0 copy-done
  3.9 0.8 dynamic-slice_bitcast_fusion.table_ref
  4.7 0.6 collective-permute-done.1.kind_ref
  5.3 0.0 copy-start.8
  5.3 0.0 collective-permute-done.2.where_ref
  5.3 0.0 copy-start.10
  5.3 0.0 collective-permute-done.surf_ref
  5.3 0.8 copy-done.8
  6.1 0.0 copy-done.10
  6.1 0.0 copy-start.7
  6.1 0.8 copy-done.7
  6.9 12.9 %shard_map.142 = bf16[16,208,256]{2,1,0:T(8,128)(2,1)} custom-call(bf16[1024,256]{1,0:T(8,128)(2,1)} %copy-done.7, bf16[4,256,256]{2,1,0:T(8,128)(2,1)} %dynamic-slice_bitcast_fusion.table_ref, s32[1024,2]{1,0:T(8,128)} %copy-done.8, s32[4,1024]{1,0:T(4,128)} %copy-done.10), custom_call_target="tpu_custom_call" | custom-call | flops 6000000000 | bytes 8388608 | tf_op jit(solution)/shard_map/pallas_call | solution.py:279
  19.8 7.2 %all-to-all-start = ((bf16[16,208,256]{2,1,0:T(8,128)(2,1)}), bf16[16,208,256]{2,1,0:T(8,128)(2,1)}, u32[]{:S(2)}, u32[]{:S(2)}) async-start(bf16[16,208,256]{2,1,0:T(8,128)(2,1)} %shard_map.142), calls=%async_computation | async-start | bytes 3407872 | tf_op jit(solution)/shard_map/all_to_all | solution.py:384
  27.0 1.6 %bitcast_multiply_fusion.1 = bf16[32,32,768]{2,1,0:T(8,128)(2,1)S(1)} fusion(bf16[1,32,32,768]{3,2,1,0:T(8,128)(2,1)} %param.16, bf16[32,32]{1,0:T(8,128)(2,1)S(1)} %get-tuple-element.76), kind=kLoop, calls=%fused_computation.8 | loop fusion | flops 786432 | bytes 3147776 | tf_op jit(solution)/shard_map/mul | solution.py:370
  28.6 0.2 fusion.1
  28.8 1.5 %collective-permute-start.3 = (bf16[32,4,768]{2,1,0:T(4,128)(2,1)S(1)}, bf16[32,4,768]{2,1,0:T(4,128)(2,1)S(1)}, u32[]{:S(2)}, u32[]{:S(2)}) collective-permute-start(bf16[32,4,768]{2,1,0:T(4,128)(2,1)S(1)} %get-tuple-element.73), channel_id=1, source_target_pairs={{0,1},{1,2},{2,3},{3,0},{4,5},{5,6},{6,7},{7,4},{8,9},{9,10},{10,1... | collective-permute-start | bytes 589832 | tf_op jit(solution)/shard_map/ppermute | solution.py:352
  30.3 1.5 %collective-permute-start.4 = (bf16[32,4,768]{2,1,0:T(4,128)(2,1)S(1)}, bf16[32,4,768]{2,1,0:T(4,128)(2,1)S(1)}, u32[]{:S(2)}, u32[]{:S(2)}) collective-permute-start(bf16[32,4,768]{2,1,0:T(4,128)(2,1)S(1)} %get-tuple-element.74), channel_id=1, source_target_pairs={{1,0},{2,1},{3,2},{0,3},{5,4},{6,5},{7,6},{4,7},{9,8},{10,9},{11,1... | collective-permute-start | bytes 589832 | tf_op jit(solution)/shard_map/ppermute | solution.py:353
  31.7 8.0 %collective-permute-done.3 = bf16[32,4,768]{2,1,0:T(4,128)(2,1)S(1)} collective-permute-done((bf16[32,4,768]{2,1,0:T(4,128)(2,1)S(1)}, bf16[32,4,768]{2,1,0:T(4,128)(2,1)S(1)}, u32[]{:S(2)}, u32[]{:S(2)}) %collective-permute-start.3) | collective-permute-done | bytes 196640 | tf_op jit(solution)/shard_map/ppermute | solution.py:352
  39.8 12.7 %collective-permute-done.4 = bf16[32,4,768]{2,1,0:T(4,128)(2,1)S(1)} collective-permute-done((bf16[32,4,768]{2,1,0:T(4,128)(2,1)S(1)}, bf16[32,4,768]{2,1,0:T(4,128)(2,1)S(1)}, u32[]{:S(2)}, u32[]{:S(2)}) %collective-permute-start.4) | collective-permute-done | bytes 196640 | tf_op jit(solution)/shard_map/ppermute | solution.py:353
  52.5 0.9 pad_maximum_fusion.5
  53.4 0.0 copy-start.6
  53.4 2.0 %collective-permute-start.5 = (bf16[4,40,768]{2,1,0:T(8,128)(2,1)}, bf16[4,40,768]{2,1,0:T(8,128)(2,1)S(1)}, u32[]{:S(2)}, u32[]{:S(2)}) collective-permute-start(bf16[4,40,768]{2,1,0:T(8,128)(2,1)} %get-tuple-element.71), channel_id=1, source_target_pairs={{0,4},{4,8},{8,12},{1,5},{5,9},{9,13},{2,6},{6,10},{10,14},{3,7},{... | collective-permute-start | bytes 737288 | tf_op jit(solution)/shard_map/ppermute | solution.py:352
  55.4 3.9 %collective-permute-start.6 = (bf16[4,40,768]{2,1,0:T(8,128)(2,1)S(1)}, bf16[4,40,768]{2,1,0:T(8,128)(2,1)}, u32[]{:S(2)}, u32[]{:S(2)}) collective-permute-start(bf16[4,40,768]{2,1,0:T(8,128)(2,1)S(1)} %get-tuple-element.72), channel_id=1, source_target_pairs={{4,0},{8,4},{12,8},{5,1},{9,5},{13,9},{6,2},{10,6},{14,10},{7,3},{... | collective-permute-start | bytes 737288 | tf_op jit(solution)/shard_map/ppermute | solution.py:353
  59.4 1.4 %reshape.39.sea_ref = f32[1024,1]{1,0:T(8,128)} reshape(f32[32,32]{1,0:T(8,128)S(1)} %get-tuple-element.75) | data formatting | bytes 8192 | tf_op jit(solution)/shard_map/reshape | solution.py:394
  60.7 0.1 pad_add_fusion.1
  60.8 9.9 %collective-permute-done.5 = bf16[4,40,768]{2,1,0:T(8,128)(2,1)S(1)} collective-permute-done((bf16[4,40,768]{2,1,0:T(8,128)(2,1)}, bf16[4,40,768]{2,1,0:T(8,128)(2,1)S(1)}, u32[]{:S(2)}, u32[]{:S(2)}) %collective-permute-start.5) | collective-permute-done | bytes 245792 | tf_op jit(solution)/shard_map/ppermute | solution.py:352
  70.7 1.6 %collective-permute-done.6 = bf16[4,40,768]{2,1,0:T(8,128)(2,1)} collective-permute-done((bf16[4,40,768]{2,1,0:T(8,128)(2,1)S(1)}, bf16[4,40,768]{2,1,0:T(8,128)(2,1)}, u32[]{:S(2)}, u32[]{:S(2)}) %collective-permute-start.6) | collective-permute-done | bytes 245792 | tf_op jit(solution)/shard_map/ppermute | solution.py:353
  72.4 3.2 %pad_maximum_fusion.2 = bf16[40,40,768]{2,1,0:T(8,128)(2,1)} fusion(bf16[4,40,768]{2,1,0:T(8,128)(2,1)} %collective-permute-done.6, bf16[32,4,768]{2,1,0:T(4,128)(2,1)S(1)} %collective-permute-done.4, bf16[32,32,768]{2,1,0:T(8,128)(2,1)S(1)} %bitcast_multiply_fusion.1, bf16[32,4,768]{2,1,0:T(4,128)(2,1)S(1)} %collective-permute-done.3, ...), kind=kLoop, calls=%fused_computation.7 | loop fusion | flops 12288000 | bytes 4915200 | tf_op jit(solution)/shard_map/concatenate | solution.py:354
  75.5 0.0 copy-done.6
  75.5 46.7 %conditional.1 = (f32[1024,768]{1,0:T(8,128)}) conditional(s32[]{:T(128)} %convert_element_type.14, (bf16[1,32,32,768]{3,2,1,0:T(8,128)(2,1)}, bf16[32,32]{1,0:T(8,128)(2,1)S(1)}, s32[2]{0:T(128)S(1)}, bf16[40,40,768]{2,1,0:T(8,128)(2,1)}, bf16[768,2304]{1,0:T(8,128)(2,1)}, /*index=5*/bf16[768,768]{1,0:T(8,128)(2,1)}, bf16[768,3072]{1,0:T(8,128)(2,1)}, ...), branch_computations={%region_0.1_spmd, %region_1.2_spmd} | conditional | flops 60000788480 | bytes 36018440 | solution.py:388
  75.5 0.0 copy-start.1
  75.5 0.1 mul.4
  75.6 2.9 %bitcast_multiply_fusion.own_ref = bf16[1024,768]{1,0:T(8,128)(2,1)} fusion(bf16[1,32,32,768]{3,2,1,0:T(8,128)(2,1)} %get-tuple-element.38, bf16[1024]{0:T(1024)(128)(2,1)S(1)} %mul.4), kind=kLoop, calls=%fused_computation | loop fusion | flops 786432 | bytes 3147776 | tf_op jit(solution)/shard_map/mul | solution.py:370
  78.5 0.0 copy-done.1
  78.5 43.7 %branch_0_fun.1 = f32[1024,768]{1,0:T(8,128)} custom-call(s32[2]{0:T(128)S(1)} %get-tuple-element.36.place_ref, bf16[40,40,768]{2,1,0:T(8,128)(2,1)S(1)} %copy-done.1, bf16[1024,768]{1,0:T(8,128)(2,1)} %bitcast_multiply_fusion.own_ref, bf16[768,2304]{1,0:T(8,128)(2,1)} %get-tuple-element.52.wqkv_ref, bf16[768,768]{1,0:T(8,128)(2,1)} %get-tuple-element.53.wo_ref, ...), custom_call_target="tpu_custom_call" | custom-call | flops 60000002048 | bytes 8388608 | tf_op jit(solution)/shard_map/cond/branch_0_fun/pallas_call | solution.py:279
  122.2 0.0 all-to-all-done.got_ref
  122.2 9.2 %shard_map.143 = bf16[1024,768]{1,0:T(8,128)(2,1)} custom-call(bf16[16,208,256]{2,1,0:T(8,128)(2,1)} %all-to-all-done.got_ref, f32[1024,768]{1,0:T(8,128)} %get-tuple-element.77.core_ref, bf16[256,768]{1,0:T(8,128)(2,1)} %bitcast.34, f32[1024,1]{1,0:T(8,128)} %reshape.39.sea_ref), custom_call_target="tpu_custom_call" | custom-call | flops 6000000000 | bytes 8388608 | tf_op jit(solution)/shard_map/pallas_call | solution.py:279
  (2 shorter events, 0.0 us)
Async XLA Ops:
  0.0 3.9 %copy-start = (bf16[2,4,256,256]{3,2,1,0:T(8,128)(2,1)S(1)}, bf16[2,4,256,256]{3,2,1,0:T(8,128)(2,1)}, u32[]{:S(2)}) copy-start(bf16[2,4,256,256]{3,2,1,0:T(8,128)(2,1)} %param.26) | copy-start | bytes 3145732
  0.0 1.8 %copy-start.9 = (bf16[1,768,256]{2,1,0:T(8,128)(2,1)S(1)}, bf16[1,768,256]{2,1,0:T(8,128)(2,1)}, u32[]{:S(2)}) copy-start(bf16[1,768,256]{2,1,0:T(8,128)(2,1)} %param.24) | copy-start | bytes 1179652
  0.0 3.0 %copy-start.3 = (s32[1,1,1,1024,2]{3,4,2,1,0:T(2,128)S(1)}, s32[1,1,1,1024,2]{3,4,2,1,0:T(2,128)}, u32[]{:S(2)}) copy-start(s32[1,1,1,1024,2]{3,4,2,1,0:T(2,128)} %param.29) | copy-start | bytes 24580
  0.0 3.3 %copy-start.4 = (s32[1,1,1,1024,2]{3,4,2,1,0:T(2,128)S(1)}, s32[1,1,1,1024,2]{3,4,2,1,0:T(2,128)}, u32[]{:S(2)}) copy-start(s32[1,1,1,1024,2]{3,4,2,1,0:T(2,128)} %param.28) | copy-start | bytes 24580
  0.1 3.3 %copy-start.5 = (s32[1,1,1,1024,2]{3,4,2,1,0:T(2,128)S(1)}, s32[1,1,1,1024,2]{3,4,2,1,0:T(2,128)}, u32[]{:S(2)}) copy-start(s32[1,1,1,1024,2]{3,4,2,1,0:T(2,128)} %param.27) | copy-start | bytes 24580
  2.4 2.9 %collective-permute-start = (bf16[1024,256]{1,0:T(8,128)(2,1)S(1)}, bf16[1024,256]{1,0:T(8,128)(2,1)S(1)}, u32[]{:S(2)}, u32[]{:S(2)}) collective-permute-start(bf16[1024,256]{1,0:T(8,128)(2,1)S(1)} %convolution_convert_fusion), channel_id=1, source_target_pairs={{0,16},{16,0},{1,17},{17,1},{2,18},{18,2},{3,19},{19,3},{4,20},{20... | collective-permute-start | bytes 1572872 | tf_op jit(solution)/shard_map/ppermute | solution.py:379
  3.2 2.1 %collective-permute-start.1 = (s32[1024,2]{1,0:T(8,128)S(1)}, s32[1024,2]{1,0:T(8,128)S(1)}, u32[]{:S(2)}, u32[]{:S(2)}) collective-permute-start(s32[1024,2]{1,0:T(8,128)S(1)} %bitcast.31), channel_id=1, source_target_pairs={{0,16},{16,0},{1,17},{17,1},{2,18},{18,2},{3,19},{19,3},{4,20},{20... | collective-permute-start | bytes 24584 | tf_op jit(solution)/shard_map/ppermute | solution.py:376
  3.3 2.0 %collective-permute-start.2 = (s32[4,1024]{1,0:T(4,128)S(1)}, s32[4,1024]{1,0:T(4,128)S(1)}, u32[]{:S(2)}, u32[]{:S(2)}) collective-permute-start(s32[4,1024]{1,0:T(4,128)S(1)} %pad_add_fusion), channel_id=1, source_target_pairs={{0,16},{16,0},{1,17},{17,1},{2,18},{18,2},{3,19},{19,3},{4,20},{20... | collective-permute-start | bytes 49160 | tf_op jit(solution)/shard_map/ppermute | solution.py:375
  5.3 0.8 copy-start.8
  5.3 0.8 copy-start.10
  6.1 0.8 copy-start.7
  19.8 102.4 %all-to-all-start = ((bf16[16,208,256]{2,1,0:T(8,128)(2,1)}), bf16[16,208,256]{2,1,0:T(8,128)(2,1)}, u32[]{:S(2)}, u32[]{:S(2)}) async-start(bf16[16,208,256]{2,1,0:T(8,128)(2,1)} %shard_map.142), calls=%async_computation | async-start | bytes 3407872 | tf_op jit(solution)/shard_map/all_to_all | solution.py:384
  28.8 11.0 %collective-permute-start.3 = (bf16[32,4,768]{2,1,0:T(4,128)(2,1)S(1)}, bf16[32,4,768]{2,1,0:T(4,128)(2,1)S(1)}, u32[]{:S(2)}, u32[]{:S(2)}) collective-permute-start(bf16[32,4,768]{2,1,0:T(4,128)(2,1)S(1)} %get-tuple-element.73), channel_id=1, source_target_pairs={{0,1},{1,2},{2,3},{3,0},{4,5},{5,6},{6,7},{7,4},{8,9},{9,10},{10,1... | collective-permute-start | bytes 589832 | tf_op jit(solution)/shard_map/ppermute | solution.py:352
  30.3 22.2 %collective-permute-start.4 = (bf16[32,4,768]{2,1,0:T(4,128)(2,1)S(1)}, bf16[32,4,768]{2,1,0:T(4,128)(2,1)S(1)}, u32[]{:S(2)}, u32[]{:S(2)}) collective-permute-start(bf16[32,4,768]{2,1,0:T(4,128)(2,1)S(1)} %get-tuple-element.74), channel_id=1, source_target_pairs={{1,0},{2,1},{3,2},{0,3},{5,4},{6,5},{7,6},{4,7},{9,8},{10,9},{11,1... | collective-permute-start | bytes 589832 | tf_op jit(solution)/shard_map/ppermute | solution.py:353
  53.4 22.2 %copy-start.6 = (f32[4,128]{1,0:T(4,128)S(1)}, f32[4,128]{1,0:T(4,128)}, u32[]{:S(2)}) copy-start(f32[4,128]{1,0:T(4,128)} %param.23) | copy-start | bytes 6148
  53.4 17.4 %collective-permute-start.5 = (bf16[4,40,768]{2,1,0:T(8,128)(2,1)}, bf16[4,40,768]{2,1,0:T(8,128)(2,1)S(1)}, u32[]{:S(2)}, u32[]{:S(2)}) collective-permute-start(bf16[4,40,768]{2,1,0:T(8,128)(2,1)} %get-tuple-element.71), channel_id=1, source_target_pairs={{0,4},{4,8},{8,12},{1,5},{5,9},{9,13},{2,6},{6,10},{10,14},{3,7},{... | collective-permute-start | bytes 737288 | tf_op jit(solution)/shard_map/ppermute | solution.py:352
  55.4 16.9 %collective-permute-start.6 = (bf16[4,40,768]{2,1,0:T(8,128)(2,1)S(1)}, bf16[4,40,768]{2,1,0:T(8,128)(2,1)}, u32[]{:S(2)}, u32[]{:S(2)}) collective-permute-start(bf16[4,40,768]{2,1,0:T(8,128)(2,1)S(1)} %get-tuple-element.72), channel_id=1, source_target_pairs={{4,0},{8,4},{12,8},{5,1},{9,5},{13,9},{6,2},{10,6},{14,10},{7,3},{... | collective-permute-start | bytes 737288 | tf_op jit(solution)/shard_map/ppermute | solution.py:353
  75.5 3.0 %copy-start.1 = (bf16[40,40,768]{2,1,0:T(8,128)(2,1)S(1)}, bf16[40,40,768]{2,1,0:T(8,128)(2,1)}, u32[]{:S(2)}) copy-start(bf16[40,40,768]{2,1,0:T(8,128)(2,1)} %get-tuple-element.37.x_ref) | copy-start | bytes 7372804 | tf_op jit(solution)/shard_map/cond
where the time goes:
time: 132 us; the launch traced here: 131 us
  Pallas kernels  65.8 us (50%)
  waiting for transfers between devices  32.9 us (25%)
  starting transfers between devices  17.4 us (13%)
  other arithmetic  10.3 us (8%)
  local copies, waits for them, and re-layouts  4.26 us (3%)
    pallas_call x3, Pallas kernels, call(): pl.pallas_call(kernel, out_shape=jax.ShapeDtypeStruct(shape, dtype), in_s...  65.8 us
    ppermute x2, waiting for transfers between devices, padded(): before = lax.ppermute(last, axis, up)  18 us
    ppermute x2, waiting for transfers between devices, padded(): after = lax.ppermute(first, axis, down)  14.4 us
    all_to_all x1, starting transfers between devices, local(): lax.all_to_all(outgoing, ('lat', 'lon'), split_axis=0, concat_axis=0, til...  7.18 us
    mul x3, other arithmetic, local(): initial = local_state * sea.astype(BF16)[:, :, None]  6.23 us
    ppermute x2, starting transfers between devices, padded(): after = lax.ppermute(first, axis, down)  5.4 us
    ppermute x2, starting transfers between devices, padded(): before = lax.ppermute(last, axis, up)  3.55 us
    concatenate x1, other arithmetic, padded(): return jnp.concatenate([before, x, after], axis=dim)  3.16 us
  transfers between devices with their start and end apart: 8, of which 5 were waited for; matrix products, arithmetic and copies ran while one was open for 9% of the time, Pallas kernels for 33%

commit v1 on v0

--- a/solution.py
+++ b/solution.py
@@ -14,7 +14,7 @@
 MARGIN = WIN // 2
 EPSILON = 1e-05
 RADIX = 32
-COLPAD = 48
+SIDE = 16
 LABEL_ROWS = 16
 VMEM_LIMIT = 56 * 1024 * 1024
 F32 = jnp.float32
@@ -71,47 +71,64 @@
             total = jnp.where(kind == b, spread[b], total)
         links_ref[t * entries : (t + 1) * entries, :] = total.astype(BF16)
 
+    many = 4
+
     def body(g, carry):
-        spot = iota((cap, entries), 0) + g * cap
+        spot = iota((many * cap, entries), 0) + g * many * cap
         pick = jnp.concatenate([onehot(spot == position[t]) for t in range(2)], axis=1)
         rows = jnp.dot(pick, links_ref[...], preferred_element_type=F32)
-        out_ref[g, 0:cap, :] = rows.astype(BF16)
         labels = lax.dot_general(
             jnp.concatenate(label, axis=1), pick, NT, preferred_element_type=F32
         ).astype(BF16)
-        out_ref[g, cap:padded_cap, :] = jnp.zeros((LABEL_ROWS, feat), BF16)
-        out_ref[g, cap:padded_cap, 0:cap] = labels
-        return carry
-
-    lax.fori_loop(0, groups, body, 0)
+        for m in range(many):
+            cut = slice(m * cap, (m + 1) * cap)
+            out_ref[g * many + m, 0:cap, :] = rows[cut].astype(BF16)
+            out_ref[g * many + m, cap:padded_cap, :] = jnp.zeros((LABEL_ROWS, feat), BF16)
+            out_ref[g * many + m, cap:padded_cap, 0:cap] = labels[:, cut]
+        return carry
+
+    lax.fori_loop(0, groups // many, body, 0)
 
 
 def finish_kernel(got_ref, core_ref, wf_ref, sea_ref, out_ref):
     groups, padded_cap, feat = got_ref.shape
     cap = padded_cap - LABEL_ROWS
-    entries = core_ref.shape[0]
+    height, breadth, _ = out_ref.shape
+    entries = height * breadth
     step = 256
     labels = []
     for g in range(groups):
         both = got_ref[g, cap:padded_cap, 0:cap].astype(F32)
         labels.append((both[0:1] * RADIX + both[1:2] - 1.0).astype(jnp.int32))
-
+    rows = jnp.concatenate([got_ref[g, 0:cap, :] for g in range(groups)], axis=0)
     for i in range(entries // step):
         entry = iota((step, cap), 0) + i * step
-        total = jnp.zeros((step, feat), F32)
-        for g in range(groups):
-            total = total + jnp.dot(
-                onehot(entry == labels[g]), got_ref[g, 0:cap, :], preferred_element_type=F32
-            )
+        pick = jnp.concatenate([onehot(entry == label) for label in labels], axis=1)
+        total = jnp.dot(pick, rows, preferred_element_type=F32)
         inject = jnp.dot(total.astype(BF16), wf_ref[...], preferred_element_type=F32)
-        rows = slice(i * step, (i + 1) * step)
-        out_ref[rows, :] = ((core_ref[rows, :] + inject) * sea_ref[rows, :]).astype(BF16)
-
-
-def conv_kernel(place_ref, x_ref, w_ref, b_ref, out_ref, even_ref, odd_ref):
-    ext_rows, cols, width = x_ref.shape
+        for k in range(step // breadth):
+            r = i * (step // breadth) + k
+            at = slice(k * breadth, (k + 1) * breadth)
+            core = core_ref[r * breadth : (r + 1) * breadth, :]
+            out_ref[r] = ((core + inject[at]) * sea_ref[:, r : r + 1]).astype(BF16)
+
+
+def conv_kernel(
+    place_ref, own_ref, side_ref, top_ref, bottom_ref, taps_ref, b_ref, out_ref,
+    even_ref, odd_ref, w_ref,
+):
+    ext_rows, cols, _ = even_ref.shape
     layers = w_ref.shape[0]
-    height, breadth, _ = out_ref.shape
+    height, breadth, width = out_ref.shape
+    for layer in range(layers):
+        for dy in range(3):
+            for i in range(4):
+                for o in range(2):
+                    tap = jnp.zeros((OCH, OCH), BF16)
+                    if 0 <= i - o <= 2:
+                        tap = taps_ref[layer, dy, i - o]
+                    at = (4 * dy + i) * OCH
+                    w_ref[layer, at : at + OCH, o * OCH : (o + 1) * OCH] = tap
     first_row, grid_rows = place_ref[0], place_ref[1]
     pairs = PACK // 2
 
@@ -121,19 +138,24 @@
         dst[row, :, 0:OCH] = left
         dst[row, :, OCH + width :] = right
 
-    def fill(r, carry):
-        row = x_ref[r]
+    def fill(r, row):
         even_ref[r, :, OCH : OCH + width] = row
         put(even_ref, r, row[:, 0:OCH], row[:, width - OCH :])
-        return carry
-
-    lax.fori_loop(MARGIN - layers, ext_rows - MARGIN + layers, fill, 0)
+
+    def middle(r, carry):
+        fill(r + MARGIN, jnp.concatenate([own_ref[r], side_ref[r]], axis=0))
+        return carry
+
+    for r in range(MARGIN):
+        fill(r, top_ref[r])
+        fill(height + MARGIN + r, bottom_ref[r])
+    lax.fori_loop(0, height, middle, 0)
     block = 2
     for layer in range(layers):
         src, dst = (even_ref, odd_ref) if layer % 2 == 0 else (odd_ref, even_ref)
         start = MARGIN - layers + layer + 1
         steps = (ext_rows - 2 * start) // block
-        bias = b_ref[layer : layer + 1, :]
+        bias = jnp.concatenate([b_ref[layer : layer + 1, :]] * 2, axis=1)
 
         def body(i, carry, layer=layer, src=src, dst=dst, start=start, bias=bias):
             base = start + i * block
@@ -174,14 +196,27 @@
 
 
 def attend_kernel(
-    place_ref, x_ref, own_ref, wqkv_ref, wo_ref, wu_ref, wd_ref, out_ref,
+    place_ref, own_ref, side_ref, top_ref, bottom_ref, wqkv_ref, wo_ref, wu_ref, wd_ref, out_ref,
     normed_ref, qkv_ref, wide_ref, att_ref,
 ):
-    ext_rows, ext_cols, width = x_ref.shape
+    ext_rows, _, width = wide_ref.shape
+    ext_cols = own_ref.shape[1] + 2 * MARGIN
     win_rows, win_cols = ext_rows // WIN, ext_cols // WIN
     size = WIN * WIN
     height, breadth = ext_rows - 2 * MARGIN, ext_cols - 2 * MARGIN
     first_row, grid_rows = place_ref[0], place_ref[1]
+
+    def fill(r, row):
+        wide_ref[r] = pltpu.roll(normalize(row.astype(F32)), MARGIN, 0)
+
+    def middle(r, carry):
+        fill(r + MARGIN, jnp.concatenate([own_ref[r], side_ref[r]], axis=0))
+        return carry
+
+    for r in range(MARGIN):
+        fill(r, top_ref[r])
+        fill(height + MARGIN + r, bottom_ref[r])
+    lax.fori_loop(0, height, middle, 0)
     heads = 4
     lanes = heads * HEAD
     lane_head = iota((size, lanes), 1) // HEAD
@@ -191,12 +226,12 @@
         for wc in range(win_cols):
             tokens = jnp.concatenate(
                 [
-                    x_ref[wr * WIN + r, wc * WIN : (wc + 1) * WIN, :].astype(F32)
+                    wide_ref[wr * WIN + r, wc * WIN : (wc + 1) * WIN, :]
                     for r in range(WIN)
                 ],
                 axis=0,
             )
-            normed_ref[wc * size : (wc + 1) * size, :] = normalize(tokens).astype(BF16)
+            normed_ref[wc * size : (wc + 1) * size, :] = tokens.astype(BF16)
         part = width
         for c in range(3):
             qkv = jnp.dot(
@@ -258,8 +293,9 @@
 
     def mlp(i, carry):
         rows = pl.ds(pl.multiple_of(i * step, step), step)
+        tokens = own_ref[pl.ds(i * (step // breadth), step // breadth)].reshape(step, width)
         projected = jnp.dot(att_ref[rows, :], wo_ref[...], preferred_element_type=F32)
-        first = (own_ref[rows, :].astype(F32) + projected).astype(BF16).astype(F32)
+        first = (tokens.astype(F32) + projected).astype(BF16).astype(F32)
         second = normalize(first).astype(BF16)
         total = first
         for c in range(hid // chunk):
@@ -287,47 +323,31 @@
     )(*args)
 
 
-def pair_weights(conv_weight):
-    layers = conv_weight.shape[0]
-    zero = jnp.zeros_like(conv_weight[:, :, 0])
-    w = [conv_weight[:, :, dx] for dx in range(3)]
-    left = jnp.concatenate([w[0], w[1], w[2], zero], axis=2)
-    right = jnp.concatenate([zero, w[0], w[1], w[2]], axis=2)
-    return jnp.concatenate([left, right], axis=3).reshape(layers, 3 * 4 * OCH, 2 * OCH)
-
-
-def convolve(extended, place, conv_weight, conv_bias):
-    ext_rows, ext_cols, width = extended.shape
-    height, breadth = ext_rows - 2 * MARGIN, ext_cols - 2 * MARGIN
-    x = jnp.concatenate(
-        [
-            extended[:, MARGIN:],
-            jnp.zeros((ext_rows, COLPAD - ext_cols, width), BF16),
-            extended[:, :MARGIN],
-        ],
-        axis=1,
-    )
-    bias = jnp.concatenate([conv_bias, conv_bias], axis=1)
-    scratch = [VMEM((ext_rows, COLPAD, width + 2 * OCH), BF16)] * 2
+def convolve(pieces, place, conv_weight, conv_bias):
+    height, breadth, width = pieces[0].shape
+    cols = pieces[2].shape[1]
+    scratch = [VMEM((height + 2 * MARGIN, cols, width + 2 * OCH), BF16)] * 2
+    scratch.append(VMEM((conv_weight.shape[0], 12 * OCH, 2 * OCH), BF16))
     core = call(
         conv_kernel, (height, breadth, width), F32,
-        (place, x, pair_weights(conv_weight), bias), scratch, 40 * 10**9, True,
+        (place, *pieces, conv_weight, conv_bias), scratch, 40 * 10**9, True,
     )
     return core.reshape(height * breadth, width)
 
 
-def attend(extended, own, place, w_qkv, w_attn_out, w_up, w_down):
-    ext_rows, ext_cols, width = extended.shape
-    entries = own.shape[0]
+def attend(pieces, place, w_qkv, w_attn_out, w_up, w_down):
+    height, breadth, width = pieces[0].shape
+    cols = pieces[2].shape[1]
+    entries, tokens = height * breadth, (breadth + 2 * MARGIN) * WIN
     scratch = [
-        VMEM((ext_cols * WIN, width), BF16),
-        VMEM((ext_cols * WIN, 3 * width), BF16),
-        VMEM((ext_rows, ext_cols, width), F32),
+        VMEM((tokens, width), BF16),
+        VMEM((tokens, 3 * width), BF16),
+        VMEM((height + 2 * MARGIN, cols, width), F32),
         VMEM((entries, width), BF16),
     ]
     return call(
         attend_kernel, (entries, width), F32,
-        (place, extended, own, w_qkv, w_attn_out, w_up, w_down), scratch, 60 * 10**9, True,
+        (place, *pieces, w_qkv, w_attn_out, w_up, w_down), scratch, 60 * 10**9, True,
     )
 
 
@@ -340,18 +360,24 @@
 
 
 def finish(got, core, w_forcing, sea):
-    return call(finish_kernel, core.shape, BF16, (got, core, w_forcing, sea), [], 6 * 10**9)
-
-
-def padded(x, axis, dim, width, wrap):
+    shape = (sea.shape[1], sea.shape[0], core.shape[1])
+    return call(finish_kernel, shape, BF16, (got, core, w_forcing, sea), [], 6 * 10**9)
+
+
+def neighbours(x, axis, dim, wrap):
     peers, length = (lax.axis_size(axis), x.shape[dim])
     up = [(i, (i + 1) % peers) for i in range(peers if wrap else peers - 1)]
     down = [(j, i) for i, j in up]
-    last = lax.slice_in_dim(x, length - width, length, axis=dim)
-    first = lax.slice_in_dim(x, 0, width, axis=dim)
-    before = lax.ppermute(last, axis, up)
-    after = lax.ppermute(first, axis, down)
-    return jnp.concatenate([before, x, after], axis=dim)
+    last = lax.slice_in_dim(x, length - MARGIN, length, axis=dim)
+    first = lax.slice_in_dim(x, 0, MARGIN, axis=dim)
+    return lax.ppermute(last, axis, up), lax.ppermute(first, axis, down)
+
+
+def edges(initial):
+    height, _, width = initial.shape
+    west, east = neighbours(initial, "lon", 1, True)
+    gap = jnp.zeros((height, SIDE - 2 * MARGIN, width), BF16)
+    return jnp.concatenate([east, gap, west], axis=1)
 
 
 def local(
@@ -367,31 +393,33 @@
     top = routes.shape[-1]
     capacity = 3 * entries * top // (2 * groups)
     sea = jnp.where(is_ocean, sea_mask, 1)
-    initial = local_state * sea.astype(BF16)[:, :, None]
+    initial = lax.optimization_barrier(local_state * sea.astype(BF16)[:, :, None])
     swap = [(0, 1), (1, 0)]
     where = jnp.concatenate(
         [routes.reshape(entries, top).T, dest_entry.reshape(entries, top).T], axis=0
     )
     where = lax.ppermute(where, "comp", swap)
     kind = lax.ppermute(block_index.reshape(entries, top), "comp", swap)
-    own = initial.reshape(entries, width)
-    surface = jnp.dot(own, w_surface[0], preferred_element_type=F32).astype(BF16)
+    side = edges(initial)
+    surface = jnp.dot(initial.reshape(entries, width), w_surface[0], preferred_element_type=F32).astype(BF16)
     surface = lax.ppermute(surface, "comp", swap)
-    lon_wide = padded(initial, "lon", 1, MARGIN, True)
-    extended = padded(lon_wide, "lat", 0, MARGIN, False)
+    surface, side = lax.optimization_barrier((surface, side))
+    ends = [jnp.concatenate([initial[a], side[a]], axis=1) for a in (slice(0, MARGIN), slice(height - MARGIN, height))]
+    top, bottom = neighbours(jnp.concatenate(ends, axis=0), "lat", 0, False)
     table = lax.dynamic_index_in_dim(regrid_blocks, 1 - component, 0, keepdims=False)
     outgoing = pack(surface, table, kind, where, groups, capacity)
+    outgoing, top, bottom = lax.optimization_barrier((outgoing, top, bottom))
     got = lax.all_to_all(outgoing, ("lat", "lon"), split_axis=0, concat_axis=0, tiled=True)
     first_row = lax.axis_index("lat") * height - MARGIN
     grid_rows = height * lax.axis_size("lat")
     place = jnp.stack([first_row, jnp.full_like(first_row, grid_rows)]).astype(jnp.int32)
     core = lax.cond(
         is_ocean,
-        lambda ext: convolve(ext, place, conv_weight, conv_bias),
-        lambda ext: attend(ext, own, place, w_qkv, w_attn_out, w_up, w_down),
-        extended,
-    )
-    result = finish(got, core, w_forcing[0], sea.astype(F32).reshape(entries, 1))
+        lambda pieces: convolve(pieces, place, conv_weight, conv_bias),
+        lambda pieces: attend(pieces, place, w_qkv, w_attn_out, w_up, w_down),
+        (initial, side, top, bottom),
+    )
+    result = finish(got, core, w_forcing[0], sea.astype(F32).T)
     return result.reshape(1, height, breadth, width)
 
 

time: 132 us -> 104 us (0.79)
  waiting for transfers between devices: 32.9 us -> 6.05 us
  other arithmetic: 10.3 us -> 4.51 us
  Pallas kernels: 65.8 us -> 68.4 us
  local copies, waits for them, and re-layouts: 4.26 us -> 5.71 us
    ppermute x4, waiting for transfers between devices: 32.3 us -> 6.04 us  [neighbours(): return (lax.ppermute(last, axis, up), lax.ppermute(first, axis, down))]
    mul x3 -> x1, other arithmetic: 6.23 us -> 1.67 us  [local(): local_state * sea.astype(BF16)[:, :, None]]
    unnamed x19 -> x14, local copies, waits for them, and re-layouts: 1.83 us -> 4.5 us
    pallas_call x3, Pallas kernels: 65.8 us -> 68.4 us  [call(): pl.pallas_call(kernel, out_shape=jax.ShapeDtypeStruct(shape, dtype), in_s...]
    concatenate x1 -> x3, other arithmetic: 3.16 us -> 1.34 us  [the longest x1 1.3 us: edges(): return jnp.concatenate([east, gap, west], axis=1)]
    reshape x1 -> x0, local copies, waits for them, and re-layouts: 1.35 us -> none  [local(): sea.astype(F32).reshape(entries, 1)]
  transfers between devices with their start and end apart: 8 -> 8, of which waited for: 5 -> 2; matrix products, arithmetic and copies ran while one was open for 9% -> 9% of each run, Pallas kernels for 33% -> 59%
where the time goes in v1:
time: 104 us; the launch traced here: 103 us
  Pallas kernels  68.4 us (66%)
  starting transfers between devices  16.4 us (16%)
  waiting for transfers between devices  6.05 us (6%)
  local copies, waits for them, and re-layouts  5.71 us (5%)
  other arithmetic  4.51 us (4%)
  matrix products  1.37 us (1%)
    pallas_call x3, Pallas kernels, call(): pl.pallas_call(kernel, out_shape=jax.ShapeDtypeStruct(shape, dtype), in_s...  68.4 us
    ppermute x4, starting transfers between devices, neighbours(): return (lax.ppermute(last, axis, up), lax.ppermute(first, axis, down))  7.94 us
    all_to_all x1, starting transfers between devices, local(): lax.all_to_all(outgoing, ('lat', 'lon'), split_axis=0, concat_axis=0, til...  7.91 us
    ppermute x4, waiting for transfers between devices, neighbours(): return (lax.ppermute(last, axis, up), lax.ppermute(first, axis, down))  6.04 us
    unnamed x14, local copies, waits for them, and re-layouts  4.5 us
  transfers between devices with their start and end apart: 8, of which 2 were waited for; matrix products, arithmetic and copies ran while one was open for 9% of the time, Pallas kernels for 59%

profile of v1, /device:TPU:12, one launch (start us, length us, event | category | flops | bytes accessed | tf_op | source)
XLA Modules:
  0.0 102.5 jit_solution(6593540443998782539)
XLA Ops:
  0.0 0.0 copy-start
  0.0 0.8 pad_add_fusion
  0.8 0.1 collective-permute-start.4
  0.9 1.7 %copy.23 = s32[1,1,1,1024,2]{4,3,2,1,0:T(8,128)} copy(s32[1,1,1,1024,2]{3,4,2,1,0:T(2,128)} %param.29) | data formatting | bytes 16384 | tf_op args[13]
  2.6 0.5 collective-permute-start.3
  3.1 0.8 copy.21
  3.9 0.6 convert_bitcast_fusion
  4.5 0.1 copy.22
  4.6 0.0 copy-start.2
  4.6 1.7 %bitcast_multiply_fusion = bf16[32,32,768]{2,1,0:T(8,128)(2,1)S(1)} fusion(bf16[1,32,32,768]{3,2,1,0:T(8,128)(2,1)} %param.16, bf16[32,32]{1,0:T(8,128)(2,1)S(1)} %copy.22), kind=kLoop, calls=%fused_computation | loop fusion | flops 786432 | bytes 3147776 | tf_op jit(solution)/shard_map/mul | solution.py:396
  6.3 0.2 fusion.2
  6.4 1.5 %collective-permute-start.1 = (bf16[32,4,768]{2,1,0:T(4,128)(2,1)S(1)}, bf16[32,4,768]{2,1,0:T(4,128)(2,1)S(1)}, u32[]{:S(2)}, u32[]{:S(2)}) collective-permute-start(bf16[32,4,768]{2,1,0:T(4,128)(2,1)S(1)} %get-tuple-element.80), channel_id=1, source_target_pairs={{1,0},{2,1},{3,2},{0,3},{5,4},{6,5},{7,6},{4,7},{9,8},{10,9},{11,1... | collective-permute-start | bytes 589832 | tf_op jit(solution)/shard_map/ppermute | solution.py:373
  7.9 0.6 collective-permute-start.2
  8.5 0.0 copy-done.2
  8.5 1.4 %convolution_convert_fusion = bf16[1024,256]{1,0:T(8,128)(2,1)} fusion(bf16[1024,768]{1,0:T(8,128)(2,1)S(1)} %bitcast.22, bf16[1,768,256]{2,1,0:T(8,128)(2,1)S(1)} %copy-done.2), kind=kOutput, calls=%fused_computation.1 | convolution fusion | flops 402915328 | bytes 2490368 | tf_op jit(solution)/shard_map/dot_general | solution.py:404
  9.9 0.0 collective-permute-start
  9.9 0.0 copy-done
  9.9 0.9 dynamic-slice_bitcast_fusion.table_ref
  10.7 0.1 pad.9.clone
  10.9 3.4 %collective-permute-done.1 = bf16[32,4,768]{2,1,0:T(4,128)(2,1)S(1)} collective-permute-done((bf16[32,4,768]{2,1,0:T(4,128)(2,1)S(1)}, bf16[32,4,768]{2,1,0:T(4,128)(2,1)S(1)}, u32[]{:S(2)}, u32[]{:S(2)}) %collective-permute-start.1) | collective-permute-done | bytes 196640 | tf_op jit(solution)/shard_map/ppermute | solution.py:373
  14.2 0.0 copy-start.1
  14.2 0.7 copy-done.1
  14.9 2.6 %collective-permute-done.2 = bf16[32,4,768]{2,1,0:T(4,128)(2,1)} collective-permute-done((bf16[32,4,768]{2,1,0:T(4,128)(2,1)S(1)}, bf16[32,4,768]{2,1,0:T(4,128)(2,1)}, u32[]{:S(2)}, u32[]{:S(2)}) %collective-permute-start.2) | collective-permute-done | bytes 196640 | tf_op jit(solution)/shard_map/ppermute | solution.py:373
  17.6 1.3 %pad_maximum_fusion = bf16[32,16,768]{2,1,0:T(8,128)(2,1)S(1)} fusion(bf16[32,4,768]{2,1,0:T(4,128)(2,1)} %collective-permute-done.2, bf16[32,4,768]{2,1,0:T(4,128)(2,1)} %copy-done.1, bf16[16]{0:T(256)(128)(2,1)S(1)} %pad.9.clone), kind=kLoop, calls=%fused_computation.2 | loop fusion | flops 2359296 | bytes 1179680 | tf_op jit(solution)/shard_map/concatenate | solution.py:380
  18.9 0.0 collective-permute-done.surf_ref
  18.9 3.5 %collective-permute-start.5 = (bf16[4,48,768]{2,1,0:T(8,128)(2,1)S(1)}, bf16[4,48,768]{2,1,0:T(8,128)(2,1)S(1)}, u32[]{:S(2)}, u32[]{:S(2)}) collective-permute-start(bf16[4,48,768]{2,1,0:T(8,128)(2,1)S(1)} %pad_maximum_fusion.1), channel_id=1, source_target_pairs={{0,4},{4,8},{8,12},{1,5},{5,9},{9,13},{2,6},{6,10},{10,14},{3,7},{... | collective-permute-start | bytes 884744 | tf_op jit(solution)/shard_map/ppermute | solution.py:373
  22.5 2.4 %collective-permute-start.6 = (bf16[4,48,768]{2,1,0:T(8,128)(2,1)S(1)}, bf16[4,48,768]{2,1,0:T(8,128)(2,1)}, u32[]{:S(2)}, u32[]{:S(2)}) collective-permute-start(bf16[4,48,768]{2,1,0:T(8,128)(2,1)S(1)} %pad_maximum_fusion.2), channel_id=1, source_target_pairs={{4,0},{8,4},{12,8},{5,1},{9,5},{13,9},{6,2},{10,6},{14,10},{7,3},{... | collective-permute-start | bytes 884744 | tf_op jit(solution)/shard_map/ppermute | solution.py:373
  24.8 0.0 collective-permute-done.3.kind_ref
  24.8 0.0 collective-permute-done.4.where_ref
  24.9 0.0 copy-start.4
  24.9 0.6 copy-done.4
  25.5 11.2 %shard_map.142 = bf16[16,208,256]{2,1,0:T(8,128)(2,1)} custom-call(bf16[1024,256]{1,0:T(8,128)(2,1)} %collective-permute-done.surf_ref, bf16[4,256,256]{2,1,0:T(8,128)(2,1)} %dynamic-slice_bitcast_fusion.table_ref, s32[1024,2]{1,0:T(8,128)} %collective-permute-done.3.kind_ref, s32[4,1024]{1,0:T(4,128)} %copy-done.4), custom_call_target="tpu_custom_call" | custom-call | flops 6000000000 | bytes 8388608 | tf_op jit(solution)/shard_map/pallas_call | solution.py:315
  36.7 0.0 copy-start.5
  36.7 0.0 collective-permute-done.5
  36.7 0.0 copy-start.3
  36.7 0.7 copy-done.3
  37.4 0.0 collective-permute-done.6
  37.4 7.9 %all-to-all-start = ((bf16[16,208,256]{2,1,0:T(8,128)(2,1)}), bf16[16,208,256]{2,1,0:T(8,128)(2,1)}, u32[]{:S(2)}, u32[]{:S(2)}) async-start(bf16[16,208,256]{2,1,0:T(8,128)(2,1)} %shard_map.142), calls=%async_computation | async-start | bytes 3407872 | tf_op jit(solution)/shard_map/all_to_all | solution.py:412
  45.3 0.1 pad_add_fusion.1
  45.4 0.0 copy-done.5
  45.4 49.0 %conditional.1 = (f32[1024,768]{1,0:T(8,128)}) conditional(s32[]{:T(128)} %convert_element_type.14, (s32[2]{0:T(128)S(1)}, bf16[32,32,768]{2,1,0:T(8,128)(2,1)S(1)}, bf16[32,16,768]{2,1,0:T(8,128)(2,1)S(1)}, bf16[4,48,768]{2,1,0:T(8,128)(2,1)}, bf16[4,48,768]{2,1,0:T(8,128)(2,1)}, /*index=5*/bf16[768,2304]{1,0:T(8,128)(2,1)}, ...), branch_computations={%region_0.1_spmd, %region_1.2_spmd} | conditional | flops 60000002048 | bytes 8388616 | solution.py:416
  45.4 49.0 %branch_0_fun.1 = f32[1024,768]{1,0:T(8,128)} custom-call(s32[2]{0:T(128)S(1)} %get-tuple-element.40.place_ref, bf16[32,32,768]{2,1,0:T(8,128)(2,1)S(1)} %get-tuple-element.41.own_ref, bf16[32,16,768]{2,1,0:T(8,128)(2,1)S(1)} %get-tuple-element.42.side_ref, bf16[4,48,768]{2,1,0:T(8,128)(2,1)} %get-tuple-element.43.top_ref, ...), custom_call_target="tpu_custom_call" | custom-call | flops 60000002048 | bytes 8388608 | tf_op jit(solution)/shard_map/cond/branch_0_fun/pallas_call | solution.py:315
  94.4 0.0 all-to-all-done.got_ref
  94.4 8.1 %shard_map.143 = bf16[32,32,768]{2,1,0:T(8,128)(2,1)} custom-call(bf16[16,208,256]{2,1,0:T(8,128)(2,1)} %all-to-all-done.got_ref, f32[1024,768]{1,0:T(8,128)} %get-tuple-element.86.core_ref, bf16[256,768]{1,0:T(8,128)(2,1)} %bitcast.25, f32[32,32]{1,0:T(8,128)} %get-tuple-element.84.sea_ref), custom_call_target="tpu_custom_call" | custom-call | flops 6000000000 | bytes 8388608 | tf_op jit(solution)/shard_map/pallas_call | solution.py:315
  (5 shorter events, 0.1 us)
Async XLA Ops:
  0.0 9.9 %copy-start = (bf16[2,4,256,256]{3,2,1,0:T(8,128)(2,1)S(1)}, bf16[2,4,256,256]{3,2,1,0:T(8,128)(2,1)}, u32[]{:S(2)}) copy-start(bf16[2,4,256,256]{3,2,1,0:T(8,128)(2,1)} %param.26) | copy-start | bytes 3145732
  0.8 24.0 %collective-permute-start.4 = (s32[4,1024]{1,0:T(4,128)S(1)}, s32[4,1024]{1,0:T(4,128)S(1)}, u32[]{:S(2)}, u32[]{:S(2)}) collective-permute-start(s32[4,1024]{1,0:T(4,128)S(1)} %pad_add_fusion), channel_id=1, source_target_pairs={{0,16},{16,0},{1,17},{17,1},{2,18},{18,2},{3,19},{19,3},{4,20},{20... | collective-permute-start | bytes 49160 | tf_op jit(solution)/shard_map/ppermute | solution.py:401
  2.6 22.2 %collective-permute-start.3 = (s32[1024,2]{1,0:T(8,128)}, s32[1024,2]{1,0:T(8,128)}, u32[]{:S(2)}, u32[]{:S(2)}) collective-permute-start(s32[1024,2]{1,0:T(8,128)} %bitcast.5), channel_id=1, source_target_pairs={{0,16},{16,0},{1,17},{17,1},{2,18},{18,2},{3,19},{19,3},{4,20},{20... | collective-permute-start | bytes 24584 | tf_op jit(solution)/shard_map/ppermute | solution.py:402
  4.6 3.9 %copy-start.2 = (bf16[1,768,256]{2,1,0:T(8,128)(2,1)S(1)}, bf16[1,768,256]{2,1,0:T(8,128)(2,1)}, u32[]{:S(2)}) copy-start(bf16[1,768,256]{2,1,0:T(8,128)(2,1)} %param.24) | copy-start | bytes 1179652
  6.4 7.8 %collective-permute-start.1 = (bf16[32,4,768]{2,1,0:T(4,128)(2,1)S(1)}, bf16[32,4,768]{2,1,0:T(4,128)(2,1)S(1)}, u32[]{:S(2)}, u32[]{:S(2)}) collective-permute-start(bf16[32,4,768]{2,1,0:T(4,128)(2,1)S(1)} %get-tuple-element.80), channel_id=1, source_target_pairs={{1,0},{2,1},{3,2},{0,3},{5,4},{6,5},{7,6},{4,7},{9,8},{10,9},{11,1... | collective-permute-start | bytes 589832 | tf_op jit(solution)/shard_map/ppermute | solution.py:373
  7.9 9.6 %collective-permute-start.2 = (bf16[32,4,768]{2,1,0:T(4,128)(2,1)S(1)}, bf16[32,4,768]{2,1,0:T(4,128)(2,1)}, u32[]{:S(2)}, u32[]{:S(2)}) collective-permute-start(bf16[32,4,768]{2,1,0:T(4,128)(2,1)S(1)} %get-tuple-element.81), channel_id=1, source_target_pairs={{0,1},{1,2},{2,3},{3,0},{4,5},{5,6},{6,7},{7,4},{8,9},{9,10},{10,1... | collective-permute-start | bytes 589832 | tf_op jit(solution)/shard_map/ppermute | solution.py:373
  9.9 9.0 %collective-permute-start = (bf16[1024,256]{1,0:T(8,128)(2,1)}, bf16[1024,256]{1,0:T(8,128)(2,1)}, u32[]{:S(2)}, u32[]{:S(2)}) collective-permute-start(bf16[1024,256]{1,0:T(8,128)(2,1)} %convolution_convert_fusion), channel_id=1, source_target_pairs={{0,16},{16,0},{1,17},{17,1},{2,18},{18,2},{3,19},{19,3},{4,20},{20... | collective-permute-start | bytes 1572872 | tf_op jit(solution)/shard_map/ppermute | solution.py:405
  14.2 0.7 copy-start.1
  18.9 17.8 %collective-permute-start.5 = (bf16[4,48,768]{2,1,0:T(8,128)(2,1)S(1)}, bf16[4,48,768]{2,1,0:T(8,128)(2,1)S(1)}, u32[]{:S(2)}, u32[]{:S(2)}) collective-permute-start(bf16[4,48,768]{2,1,0:T(8,128)(2,1)S(1)} %pad_maximum_fusion.1), channel_id=1, source_target_pairs={{0,4},{4,8},{8,12},{1,5},{5,9},{9,13},{2,6},{6,10},{10,14},{3,7},{... | collective-permute-start | bytes 884744 | tf_op jit(solution)/shard_map/ppermute | solution.py:373
  22.5 15.0 %collective-permute-start.6 = (bf16[4,48,768]{2,1,0:T(8,128)(2,1)S(1)}, bf16[4,48,768]{2,1,0:T(8,128)(2,1)}, u32[]{:S(2)}, u32[]{:S(2)}) collective-permute-start(bf16[4,48,768]{2,1,0:T(8,128)(2,1)S(1)} %pad_maximum_fusion.2), channel_id=1, source_target_pairs={{4,0},{8,4},{12,8},{5,1},{9,5},{13,9},{6,2},{10,6},{14,10},{7,3},{... | collective-permute-start | bytes 884744 | tf_op jit(solution)/shard_map/ppermute | solution.py:373
  24.9 0.6 copy-start.4
  36.7 8.7 %copy-start.5 = (f32[4,128]{1,0:T(4,128)S(1)}, f32[4,128]{1,0:T(4,128)}, u32[]{:S(2)}) copy-start(f32[4,128]{1,0:T(4,128)} %param.23) | copy-start | bytes 6148
  36.7 0.7 copy-start.3
  37.4 57.0 %all-to-all-start = ((bf16[16,208,256]{2,1,0:T(8,128)(2,1)}), bf16[16,208,256]{2,1,0:T(8,128)(2,1)}, u32[]{:S(2)}, u32[]{:S(2)}) async-start(bf16[16,208,256]{2,1,0:T(8,128)(2,1)} %shard_map.142), calls=%async_computation | async-start | bytes 3407872 | tf_op jit(solution)/shard_map/all_to_all | solution.py:412

commit v2 on v1

--- a/solution.py
+++ b/solution.py
@@ -42,7 +42,7 @@
     return jnp.where(mask, 1.0, 0.0).astype(BF16)
 
 
-def pack_kernel(surf_ref, table_ref, kind_ref, where_ref, out_ref, links_ref):
+def pack_kernel(surf_ref, table_ref, where_ref, out_ref, links_ref):
     groups, padded_cap, feat = out_ref.shape
     cap = padded_cap - LABEL_ROWS
     entries = surf_ref.shape[0]
@@ -61,11 +61,12 @@
         row = iota((LABEL_ROWS, entries), 0)
         label.append(jnp.where(row == 0, high, jnp.where(row == 1, low, 0.0)).astype(BF16))
     surf = surf_ref[...]
+    kinds = where_ref[...].astype(F32).T
     spread = [
         jnp.dot(surf, table_ref[b], preferred_element_type=F32) for b in range(table_ref.shape[0])
     ]
     for t in range(2):
-        kind = kind_ref[:, t : t + 1]
+        kind = kinds[:, 4 + t : 5 + t]
         total = jnp.where(kind == 0, spread[0], 0.0)
         for b in range(1, len(spread)):
             total = jnp.where(kind == b, spread[b], total)
@@ -196,9 +197,15 @@
 
 
 def attend_kernel(
-    place_ref, own_ref, side_ref, top_ref, bottom_ref, wqkv_ref, wo_ref, wu_ref, wd_ref, out_ref,
-    normed_ref, qkv_ref, wide_ref, att_ref,
+    place_ref, own_ref, side_ref, top_ref, bottom_ref, wqkv_ref, wo_hbm, wu_hbm, wd_hbm, out_ref,
+    normed_ref, qkv_ref, wide_ref, att_ref, wo_ref, wu_ref, wd_ref, sems,
 ):
+    loads = [
+        pltpu.make_async_copy(src, dst, sems.at[n])
+        for n, (src, dst) in enumerate(((wo_hbm, wo_ref), (wu_hbm, wu_ref), (wd_hbm, wd_ref)))
+    ]
+    for load in loads:
+        load.start()
     ext_rows, _, width = wide_ref.shape
     ext_cols = own_ref.shape[1] + 2 * MARGIN
     win_rows, win_cols = ext_rows // WIN, ext_cols // WIN
@@ -275,7 +282,7 @@
                     ] = got[r * WIN : (r + 1) * WIN]
             return carry
 
-        lax.fori_loop(0, win_cols, window, 0)
+        lax.fori_loop(0, win_cols, window, 0, unroll=True)
         return carry
 
     lax.fori_loop(0, win_rows, window_row, 0)
@@ -287,7 +294,9 @@
         return carry
 
     lax.fori_loop(0, height, gather, 0)
-    step = 256
+    for load in loads:
+        load.wait()
+    step = 512
     hid = wu_ref.shape[1]
     chunk = 768
 
@@ -308,10 +317,12 @@
     lax.fori_loop(0, height * breadth // step, mlp, 0)
 
 
-def call(kernel, shape, dtype, args, scratch, flops, smem_first=False):
+def call(kernel, shape, dtype, args, scratch, flops, smem_first=False, left=0):
     specs = [pl.BlockSpec(memory_space=VMEM) for _ in args]
     if smem_first:
         specs[0] = pl.BlockSpec(memory_space=pltpu.SMEM)
+    for n in range(len(args) - left, len(args)):
+        specs[n] = pl.BlockSpec(memory_space=pl.ANY)
     return pl.pallas_call(
         kernel,
         out_shape=jax.ShapeDtypeStruct(shape, dtype),
@@ -344,17 +355,21 @@
         VMEM((tokens, 3 * width), BF16),
         VMEM((height + 2 * MARGIN, cols, width), F32),
         VMEM((entries, width), BF16),
+        VMEM(w_attn_out.shape, BF16),
+        VMEM(w_up.shape, BF16),
+        VMEM(w_down.shape, BF16),
+        pltpu.SemaphoreType.DMA((3,)),
     ]
     return call(
         attend_kernel, (entries, width), F32,
-        (place, *pieces, w_qkv, w_attn_out, w_up, w_down), scratch, 60 * 10**9, True,
-    )
-
-
-def pack(surface, table, kind, where, groups, capacity):
+        (place, *pieces, w_qkv, w_attn_out, w_up, w_down), scratch, 60 * 10**9, True, 3,
+    )
+
+
+def pack(surface, table, where, groups, capacity):
     entries, feat = surface.shape
     return call(
-        pack_kernel, (groups, capacity + LABEL_ROWS, feat), BF16, (surface, table, kind, where),
+        pack_kernel, (groups, capacity + LABEL_ROWS, feat), BF16, (surface, table, where),
         [VMEM((2 * entries, feat), BF16)], 6 * 10**9,
     )
 
@@ -396,10 +411,9 @@
     initial = lax.optimization_barrier(local_state * sea.astype(BF16)[:, :, None])
     swap = [(0, 1), (1, 0)]
     where = jnp.concatenate(
-        [routes.reshape(entries, top).T, dest_entry.reshape(entries, top).T], axis=0
+        [a.reshape(entries, top).T for a in (routes, dest_entry, block_index, block_index)], axis=0
     )
     where = lax.ppermute(where, "comp", swap)
-    kind = lax.ppermute(block_index.reshape(entries, top), "comp", swap)
     side = edges(initial)
     surface = jnp.dot(initial.reshape(entries, width), w_surface[0], preferred_element_type=F32).astype(BF16)
     surface = lax.ppermute(surface, "comp", swap)
@@ -407,7 +421,7 @@
     ends = [jnp.concatenate([initial[a], side[a]], axis=1) for a in (slice(0, MARGIN), slice(height - MARGIN, height))]
     top, bottom = neighbours(jnp.concatenate(ends, axis=0), "lat", 0, False)
     table = lax.dynamic_index_in_dim(regrid_blocks, 1 - component, 0, keepdims=False)
-    outgoing = pack(surface, table, kind, where, groups, capacity)
+    outgoing = pack(surface, table, where, groups, capacity)
     outgoing, top, bottom = lax.optimization_barrier((outgoing, top, bottom))
     got = lax.all_to_all(outgoing, ("lat", "lon"), split_axis=0, concat_axis=0, tiled=True)
     first_row = lax.axis_index("lat") * height - MARGIN

time: 104 us -> 91.7 us (0.88); the launches traced: 103 us -> 91.3 us
  Pallas kernels: 68.4 us -> 56.8 us
  waiting for transfers between devices: 6.05 us -> 8.16 us
  local copies, waits for them, and re-layouts: 5.71 us -> 4 us
    pallas_call x3, Pallas kernels: 68.4 us -> 56.8 us  [call(): pl.pallas_call(kernel, out_shape=jax.ShapeDtypeStruct(shape, dtype), in_s...]
    unnamed x14 -> x13, local copies, waits for them, and re-layouts: 4.5 us -> 2.81 us
    all_to_all x1, waiting for transfers between devices: 0.01 us -> 1.63 us  [local(): lax.all_to_all(outgoing, ('lat', 'lon'), split_axis=0, concat_axis=0, til...]
  transfers between devices with their start and end apart: 8 -> 7, of which waited for: 2 -> 3; matrix products, arithmetic and copies ran while one was open for 9% -> 8% of each run, Pallas kernels for 59% -> 53%
where the time goes in v2:
time: 91.7 us; the launch traced here: 91.3 us
  Pallas kernels  56.8 us (62%)
  starting transfers between devices  15.9 us (17%)
  waiting for transfers between devices  8.16 us (9%)
  other arithmetic  4.55 us (5%)
  local copies, waits for them, and re-layouts  4 us (4%)
  matrix products  1.37 us (1%)
    pallas_call x3, Pallas kernels, call(): pl.pallas_call(kernel, out_shape=jax.ShapeDtypeStruct(shape, dtype), in_s...  56.8 us
    ppermute x4, starting transfers between devices, neighbours(): return (lax.ppermute(last, axis, up), lax.ppermute(first, axis, down))  7.94 us
    all_to_all x1, starting transfers between devices, local(): lax.all_to_all(outgoing, ('lat', 'lon'), split_axis=0, concat_axis=0, til...  7.91 us
    ppermute x4, waiting for transfers between devices, neighbours(): return (lax.ppermute(last, axis, up), lax.ppermute(first, axis, down))  6.52 us
    unnamed x13, local copies, waits for them, and re-layouts  2.81 us
  transfers between devices with their start and end apart: 7, of which 3 were waited for; matrix products, arithmetic and copies ran while one was open for 8% of the time, Pallas kernels for 53%

profile of v2, /device:TPU:12, one launch (start us, length us, event | category | flops | bytes accessed | tf_op | source)
XLA Modules:
  0.0 91.3 jit_solution(7835585872332869002)
XLA Ops:
  0.0 0.0 copy-start
  0.0 0.9 pad_add_fusion
  0.9 0.1 collective-permute-start.3
  0.9 0.8 copy.21
  1.7 0.6 convert_bitcast_fusion
  2.3 0.1 copy.22
  2.4 0.0 copy-start.2
  2.4 1.7 %bitcast_multiply_fusion = bf16[32,32,768]{2,1,0:T(8,128)(2,1)S(1)} fusion(bf16[1,32,32,768]{3,2,1,0:T(8,128)(2,1)} %param.16, bf16[32,32]{1,0:T(8,128)(2,1)S(1)} %copy.22), kind=kLoop, calls=%fused_computation | loop fusion | flops 786432 | bytes 3147776 | tf_op jit(solution)/shard_map/mul | solution.py:411
  4.1 0.2 fusion.2
  4.3 1.5 %collective-permute-start.1 = (bf16[32,4,768]{2,1,0:T(4,128)(2,1)S(1)}, bf16[32,4,768]{2,1,0:T(4,128)(2,1)S(1)}, u32[]{:S(2)}, u32[]{:S(2)}) collective-permute-start(bf16[32,4,768]{2,1,0:T(4,128)(2,1)S(1)} %get-tuple-element.80), channel_id=1, source_target_pairs={{1,0},{2,1},{3,2},{0,3},{5,4},{6,5},{7,6},{4,7},{9,8},{10,9},{11,1... | collective-permute-start | bytes 589832 | tf_op jit(solution)/shard_map/ppermute | solution.py:388
  5.8 0.6 collective-permute-start.2
  6.4 0.0 copy-done.2
  6.4 1.4 %convolution_convert_fusion = bf16[1024,256]{1,0:T(8,128)(2,1)} fusion(bf16[1024,768]{1,0:T(8,128)(2,1)S(1)} %bitcast.24, bf16[1,768,256]{2,1,0:T(8,128)(2,1)S(1)} %copy-done.2), kind=kOutput, calls=%fused_computation.1 | convolution fusion | flops 402915328 | bytes 2490368 | tf_op jit(solution)/shard_map/dot_general | solution.py:418
  7.7 0.0 collective-permute-start
  7.7 0.0 copy-done
  7.7 0.8 dynamic-slice_bitcast_fusion.table_ref
  8.6 0.1 pad.11.clone
  8.7 3.3 %collective-permute-done.1 = bf16[32,4,768]{2,1,0:T(4,128)(2,1)S(1)} collective-permute-done((bf16[32,4,768]{2,1,0:T(4,128)(2,1)S(1)}, bf16[32,4,768]{2,1,0:T(4,128)(2,1)S(1)}, u32[]{:S(2)}, u32[]{:S(2)}) %collective-permute-start.1) | collective-permute-done | bytes 196640 | tf_op jit(solution)/shard_map/ppermute | solution.py:388
  12.0 0.0 copy-start.1
  12.0 0.7 copy-done.1
  12.7 3.2 %collective-permute-done.2 = bf16[32,4,768]{2,1,0:T(4,128)(2,1)} collective-permute-done((bf16[32,4,768]{2,1,0:T(4,128)(2,1)S(1)}, bf16[32,4,768]{2,1,0:T(4,128)(2,1)}, u32[]{:S(2)}, u32[]{:S(2)}) %collective-permute-start.2) | collective-permute-done | bytes 196640 | tf_op jit(solution)/shard_map/ppermute | solution.py:388
  15.9 1.3 %pad_maximum_fusion = bf16[32,16,768]{2,1,0:T(8,128)(2,1)S(1)} fusion(bf16[32,4,768]{2,1,0:T(4,128)(2,1)} %collective-permute-done.2, bf16[32,4,768]{2,1,0:T(4,128)(2,1)} %copy-done.1, bf16[16]{0:T(256)(128)(2,1)S(1)} %pad.11.clone), kind=kLoop, calls=%fused_computation.2 | loop fusion | flops 2359296 | bytes 1179680 | tf_op jit(solution)/shard_map/concatenate | solution.py:395
  17.2 0.0 collective-permute-done.surf_ref
  17.2 3.5 %collective-permute-start.4 = (bf16[4,48,768]{2,1,0:T(8,128)(2,1)S(1)}, bf16[4,48,768]{2,1,0:T(8,128)(2,1)S(1)}, u32[]{:S(2)}, u32[]{:S(2)}) collective-permute-start(bf16[4,48,768]{2,1,0:T(8,128)(2,1)S(1)} %pad_maximum_fusion.1), channel_id=1, source_target_pairs={{0,4},{4,8},{8,12},{1,5},{5,9},{9,13},{2,6},{6,10},{10,14},{3,7},{... | collective-permute-start | bytes 884744 | tf_op jit(solution)/shard_map/ppermute | solution.py:388
  20.8 2.4 %collective-permute-start.5 = (bf16[4,48,768]{2,1,0:T(8,128)(2,1)S(1)}, bf16[4,48,768]{2,1,0:T(8,128)(2,1)}, u32[]{:S(2)}, u32[]{:S(2)}) collective-permute-start(bf16[4,48,768]{2,1,0:T(8,128)(2,1)S(1)} %pad_maximum_fusion.2), channel_id=1, source_target_pairs={{4,0},{8,4},{12,8},{5,1},{9,5},{13,9},{6,2},{10,6},{14,10},{7,3},{... | collective-permute-start | bytes 884744 | tf_op jit(solution)/shard_map/ppermute | solution.py:388
  23.1 0.0 collective-permute-done.3.where_ref
  23.2 0.0 copy-start.4
  23.2 0.6 copy-done.4
  23.8 11.2 %shard_map.142 = bf16[16,208,256]{2,1,0:T(8,128)(2,1)} custom-call(bf16[1024,256]{1,0:T(8,128)(2,1)} %collective-permute-done.surf_ref, bf16[4,256,256]{2,1,0:T(8,128)(2,1)} %dynamic-slice_bitcast_fusion.table_ref, s32[8,1024]{1,0:T(8,128)} %copy-done.4), custom_call_target="tpu_custom_call" | custom-call | flops 6000000000 | bytes 8388608 | tf_op jit(solution)/shard_map/pallas_call | solution.py:326
  35.0 0.0 copy-start.5
  35.0 0.0 collective-permute-done.4
  35.0 0.0 copy-start.3
  35.0 0.7 copy-done.3
  35.7 0.0 collective-permute-done.5
  35.7 7.9 %all-to-all-start = ((bf16[16,208,256]{2,1,0:T(8,128)(2,1)}), bf16[16,208,256]{2,1,0:T(8,128)(2,1)}, u32[]{:S(2)}, u32[]{:S(2)}) async-start(bf16[16,208,256]{2,1,0:T(8,128)(2,1)} %shard_map.142), calls=%async_computation | async-start | bytes 3407872 | tf_op jit(solution)/shard_map/all_to_all | solution.py:426
  43.6 0.1 pad_add_fusion.1
  43.7 0.0 copy-done.5
  43.7 37.8 %conditional.1 = (f32[1024,768]{1,0:T(8,128)}) conditional(s32[]{:T(128)} %convert_element_type.14, (s32[2]{0:T(128)S(1)}, bf16[32,32,768]{2,1,0:T(8,128)(2,1)S(1)}, bf16[32,16,768]{2,1,0:T(8,128)(2,1)S(1)}, bf16[4,48,768]{2,1,0:T(8,128)(2,1)}, bf16[4,48,768]{2,1,0:T(8,128)(2,1)}, /*index=5*/bf16[768,2304]{1,0:T(8,128)(2,1)}, ...), branch_computations={%region_0.1_spmd, %region_1.2_spmd} | conditional | flops 60000002048 | bytes 8388616 | solution.py:430
  43.8 37.5 %branch_0_fun.1 = f32[1024,768]{1,0:T(8,128)} custom-call(s32[2]{0:T(128)S(1)} %get-tuple-element.40.place_ref, bf16[32,32,768]{2,1,0:T(8,128)(2,1)S(1)} %get-tuple-element.41.own_ref, bf16[32,16,768]{2,1,0:T(8,128)(2,1)S(1)} %get-tuple-element.42.side_ref, bf16[4,48,768]{2,1,0:T(8,128)(2,1)} %get-tuple-element.43.top_ref, ...), custom_call_target="tpu_custom_call" | custom-call | flops 60000002048 | bytes 8388608 | tf_op jit(solution)/shard_map/cond/branch_0_fun/pallas_call | solution.py:326
  81.5 1.6 %all-to-all-done.got_ref = bf16[16,208,256]{2,1,0:T(8,128)(2,1)} async-done(((bf16[16,208,256]{2,1,0:T(8,128)(2,1)}), bf16[16,208,256]{2,1,0:T(8,128)(2,1)}, u32[]{:S(2)}, u32[]{:S(2)}) %all-to-all-start) | async-done | bytes 1703968 | tf_op jit(solution)/shard_map/all_to_all | solution.py:426
  83.2 8.1 %shard_map.143 = bf16[32,32,768]{2,1,0:T(8,128)(2,1)} custom-call(bf16[16,208,256]{2,1,0:T(8,128)(2,1)} %all-to-all-done.got_ref, f32[1024,768]{1,0:T(8,128)} %get-tuple-element.86.core_ref, bf16[256,768]{1,0:T(8,128)(2,1)} %bitcast.28, f32[32,32]{1,0:T(8,128)} %get-tuple-element.84.sea_ref), custom_call_target="tpu_custom_call" | custom-call | flops 6000000000 | bytes 8388608 | tf_op jit(solution)/shard_map/pallas_call | solution.py:326
  (5 shorter events, 0.1 us)
Async XLA Ops:
  0.0 7.7 %copy-start = (bf16[2,4,256,256]{3,2,1,0:T(8,128)(2,1)S(1)}, bf16[2,4,256,256]{3,2,1,0:T(8,128)(2,1)}, u32[]{:S(2)}) copy-start(bf16[2,4,256,256]{3,2,1,0:T(8,128)(2,1)} %param.26) | copy-start | bytes 3145732
  0.9 22.3 %collective-permute-start.3 = (s32[8,1024]{1,0:T(8,128)S(1)}, s32[8,1024]{1,0:T(8,128)S(1)}, u32[]{:S(2)}, u32[]{:S(2)}) collective-permute-start(s32[8,1024]{1,0:T(8,128)S(1)} %pad_add_fusion), channel_id=1, source_target_pairs={{0,16},{16,0},{1,17},{17,1},{2,18},{18,2},{3,19},{19,3},{4,20},{20... | collective-permute-start | bytes 98312 | tf_op jit(solution)/shard_map/ppermute | solution.py:416
  2.4 3.9 %copy-start.2 = (bf16[1,768,256]{2,1,0:T(8,128)(2,1)S(1)}, bf16[1,768,256]{2,1,0:T(8,128)(2,1)}, u32[]{:S(2)}) copy-start(bf16[1,768,256]{2,1,0:T(8,128)(2,1)} %param.24) | copy-start | bytes 1179652
  4.3 7.7 %collective-permute-start.1 = (bf16[32,4,768]{2,1,0:T(4,128)(2,1)S(1)}, bf16[32,4,768]{2,1,0:T(4,128)(2,1)S(1)}, u32[]{:S(2)}, u32[]{:S(2)}) collective-permute-start(bf16[32,4,768]{2,1,0:T(4,128)(2,1)S(1)} %get-tuple-element.80), channel_id=1, source_target_pairs={{1,0},{2,1},{3,2},{0,3},{5,4},{6,5},{7,6},{4,7},{9,8},{10,9},{11,1... | collective-permute-start | bytes 589832 | tf_op jit(solution)/shard_map/ppermute | solution.py:388
  5.8 10.1 %collective-permute-start.2 = (bf16[32,4,768]{2,1,0:T(4,128)(2,1)S(1)}, bf16[32,4,768]{2,1,0:T(4,128)(2,1)}, u32[]{:S(2)}, u32[]{:S(2)}) collective-permute-start(bf16[32,4,768]{2,1,0:T(4,128)(2,1)S(1)} %get-tuple-element.81), channel_id=1, source_target_pairs={{0,1},{1,2},{2,3},{3,0},{4,5},{5,6},{6,7},{7,4},{8,9},{9,10},{10,1... | collective-permute-start | bytes 589832 | tf_op jit(solution)/shard_map/ppermute | solution.py:388
  7.7 9.5 %collective-permute-start = (bf16[1024,256]{1,0:T(8,128)(2,1)}, bf16[1024,256]{1,0:T(8,128)(2,1)}, u32[]{:S(2)}, u32[]{:S(2)}) collective-permute-start(bf16[1024,256]{1,0:T(8,128)(2,1)} %convolution_convert_fusion), channel_id=1, source_target_pairs={{0,16},{16,0},{1,17},{17,1},{2,18},{18,2},{3,19},{19,3},{4,20},{20... | collective-permute-start | bytes 1572872 | tf_op jit(solution)/shard_map/ppermute | solution.py:419
  12.0 0.7 copy-start.1
  17.2 17.7 %collective-permute-start.4 = (bf16[4,48,768]{2,1,0:T(8,128)(2,1)S(1)}, bf16[4,48,768]{2,1,0:T(8,128)(2,1)S(1)}, u32[]{:S(2)}, u32[]{:S(2)}) collective-permute-start(bf16[4,48,768]{2,1,0:T(8,128)(2,1)S(1)} %pad_maximum_fusion.1), channel_id=1, source_target_pairs={{0,4},{4,8},{8,12},{1,5},{5,9},{9,13},{2,6},{6,10},{10,14},{3,7},{... | collective-permute-start | bytes 884744 | tf_op jit(solution)/shard_map/ppermute | solution.py:388
  20.8 14.9 %collective-permute-start.5 = (bf16[4,48,768]{2,1,0:T(8,128)(2,1)S(1)}, bf16[4,48,768]{2,1,0:T(8,128)(2,1)}, u32[]{:S(2)}, u32[]{:S(2)}) collective-permute-start(bf16[4,48,768]{2,1,0:T(8,128)(2,1)S(1)} %pad_maximum_fusion.2), channel_id=1, source_target_pairs={{4,0},{8,4},{12,8},{5,1},{9,5},{13,9},{6,2},{10,6},{14,10},{7,3},{... | collective-permute-start | bytes 884744 | tf_op jit(solution)/shard_map/ppermute | solution.py:388
  23.2 0.6 copy-start.4
  35.0 8.7 %copy-start.5 = (f32[4,128]{1,0:T(4,128)S(1)}, f32[4,128]{1,0:T(4,128)}, u32[]{:S(2)}) copy-start(f32[4,128]{1,0:T(4,128)} %param.23) | copy-start | bytes 6148
  35.0 0.7 copy-start.3
  35.7 47.5 %all-to-all-start = ((bf16[16,208,256]{2,1,0:T(8,128)(2,1)}), bf16[16,208,256]{2,1,0:T(8,128)(2,1)}, u32[]{:S(2)}, u32[]{:S(2)}) async-start(bf16[16,208,256]{2,1,0:T(8,128)(2,1)} %shard_map.142), calls=%async_computation | async-start | bytes 3407872 | tf_op jit(solution)/shard_map/all_to_all | solution.py:426

commit v3 on v2

--- a/solution.py
+++ b/solution.py
@@ -72,7 +72,7 @@
             total = jnp.where(kind == b, spread[b], total)
         links_ref[t * entries : (t + 1) * entries, :] = total.astype(BF16)
 
-    many = 4
+    many = 8
 
     def body(g, carry):
         spot = iota((many * cap, entries), 0) + g * many * cap
@@ -96,7 +96,7 @@
     cap = padded_cap - LABEL_ROWS
     height, breadth, _ = out_ref.shape
     entries = height * breadth
-    step = 256
+    step = 512
     labels = []
     for g in range(groups):
         both = got_ref[g, cap:padded_cap, 0:cap].astype(F32)

time: 91.7 us -> 91.1 us (level)
  no operation moved by 1% of the time
where the time goes in v3:
time: 91.1 us; the launch traced here: 90.7 us
  Pallas kernels  56.2 us (62%)
  starting transfers between devices  15.9 us (17%)
  waiting for transfers between devices  8.16 us (9%)
  other arithmetic  4.55 us (5%)
  local copies, waits for them, and re-layouts  4 us (4%)
  matrix products  1.37 us (2%)
    pallas_call x3, Pallas kernels, call(): pl.pallas_call(kernel, out_shape=jax.ShapeDtypeStruct(shape, dtype), in_s...  56.2 us
    ppermute x4, starting transfers between devices, neighbours(): return (lax.ppermute(last, axis, up), lax.ppermute(first, axis, down))  7.94 us
    all_to_all x1, starting transfers between devices, local(): lax.all_to_all(outgoing, ('lat', 'lon'), split_axis=0, concat_axis=0, til...  7.91 us
    ppermute x4, waiting for transfers between devices, neighbours(): return (lax.ppermute(last, axis, up), lax.ppermute(first, axis, down))  6.52 us
    unnamed x13, local copies, waits for them, and re-layouts  2.81 us
  transfers between devices with their start and end apart: 7, of which 3 were waited for; matrix products, arithmetic and copies ran while one was open for 8% of the time, Pallas kernels for 53%

profile of v3, /device:TPU:12, one launch (start us, length us, event | category | flops | bytes accessed | tf_op | source)
XLA Modules:
  0.0 90.7 jit_solution(5698294281217858833)
XLA Ops:
  0.0 0.0 copy-start
  0.0 0.9 pad_add_fusion
  0.9 0.1 collective-permute-start.3
  0.9 0.8 copy.21
  1.7 0.6 convert_bitcast_fusion
  2.3 0.1 copy.22
  2.4 0.0 copy-start.2
  2.4 1.7 %bitcast_multiply_fusion = bf16[32,32,768]{2,1,0:T(8,128)(2,1)S(1)} fusion(bf16[1,32,32,768]{3,2,1,0:T(8,128)(2,1)} %param.16, bf16[32,32]{1,0:T(8,128)(2,1)S(1)} %copy.22), kind=kLoop, calls=%fused_computation | loop fusion | flops 786432 | bytes 3147776 | tf_op jit(solution)/shard_map/mul | solution.py:411
  4.1 0.2 fusion.2
  4.3 1.5 %collective-permute-start.1 = (bf16[32,4,768]{2,1,0:T(4,128)(2,1)S(1)}, bf16[32,4,768]{2,1,0:T(4,128)(2,1)S(1)}, u32[]{:S(2)}, u32[]{:S(2)}) collective-permute-start(bf16[32,4,768]{2,1,0:T(4,128)(2,1)S(1)} %get-tuple-element.80), channel_id=1, source_target_pairs={{1,0},{2,1},{3,2},{0,3},{5,4},{6,5},{7,6},{4,7},{9,8},{10,9},{11,1... | collective-permute-start | bytes 589832 | tf_op jit(solution)/shard_map/ppermute | solution.py:388
  5.8 0.6 collective-permute-start.2
  6.4 0.0 copy-done.2
  6.4 1.4 %convolution_convert_fusion = bf16[1024,256]{1,0:T(8,128)(2,1)} fusion(bf16[1024,768]{1,0:T(8,128)(2,1)S(1)} %bitcast.24, bf16[1,768,256]{2,1,0:T(8,128)(2,1)S(1)} %copy-done.2), kind=kOutput, calls=%fused_computation.1 | convolution fusion | flops 402915328 | bytes 2490368 | tf_op jit(solution)/shard_map/dot_general | solution.py:418
  7.7 0.0 collective-permute-start
  7.7 0.0 copy-done
  7.7 0.8 dynamic-slice_bitcast_fusion.table_ref
  8.6 0.1 pad.11.clone
  8.7 3.3 %collective-permute-done.1 = bf16[32,4,768]{2,1,0:T(4,128)(2,1)S(1)} collective-permute-done((bf16[32,4,768]{2,1,0:T(4,128)(2,1)S(1)}, bf16[32,4,768]{2,1,0:T(4,128)(2,1)S(1)}, u32[]{:S(2)}, u32[]{:S(2)}) %collective-permute-start.1) | collective-permute-done | bytes 196640 | tf_op jit(solution)/shard_map/ppermute | solution.py:388
  12.0 0.0 copy-start.1
  12.0 0.7 copy-done.1
  12.7 3.2 %collective-permute-done.2 = bf16[32,4,768]{2,1,0:T(4,128)(2,1)} collective-permute-done((bf16[32,4,768]{2,1,0:T(4,128)(2,1)S(1)}, bf16[32,4,768]{2,1,0:T(4,128)(2,1)}, u32[]{:S(2)}, u32[]{:S(2)}) %collective-permute-start.2) | collective-permute-done | bytes 196640 | tf_op jit(solution)/shard_map/ppermute | solution.py:388
  15.9 1.3 %pad_maximum_fusion = bf16[32,16,768]{2,1,0:T(8,128)(2,1)S(1)} fusion(bf16[32,4,768]{2,1,0:T(4,128)(2,1)} %collective-permute-done.2, bf16[32,4,768]{2,1,0:T(4,128)(2,1)} %copy-done.1, bf16[16]{0:T(256)(128)(2,1)S(1)} %pad.11.clone), kind=kLoop, calls=%fused_computation.2 | loop fusion | flops 2359296 | bytes 1179680 | tf_op jit(solution)/shard_map/concatenate | solution.py:395
  17.2 0.0 collective-permute-done.surf_ref
  17.2 3.5 %collective-permute-start.4 = (bf16[4,48,768]{2,1,0:T(8,128)(2,1)S(1)}, bf16[4,48,768]{2,1,0:T(8,128)(2,1)S(1)}, u32[]{:S(2)}, u32[]{:S(2)}) collective-permute-start(bf16[4,48,768]{2,1,0:T(8,128)(2,1)S(1)} %pad_maximum_fusion.1), channel_id=1, source_target_pairs={{0,4},{4,8},{8,12},{1,5},{5,9},{9,13},{2,6},{6,10},{10,14},{3,7},{... | collective-permute-start | bytes 884744 | tf_op jit(solution)/shard_map/ppermute | solution.py:388
  20.8 2.4 %collective-permute-start.5 = (bf16[4,48,768]{2,1,0:T(8,128)(2,1)S(1)}, bf16[4,48,768]{2,1,0:T(8,128)(2,1)}, u32[]{:S(2)}, u32[]{:S(2)}) collective-permute-start(bf16[4,48,768]{2,1,0:T(8,128)(2,1)S(1)} %pad_maximum_fusion.2), channel_id=1, source_target_pairs={{4,0},{8,4},{12,8},{5,1},{9,5},{13,9},{6,2},{10,6},{14,10},{7,3},{... | collective-permute-start | bytes 884744 | tf_op jit(solution)/shard_map/ppermute | solution.py:388
  23.1 0.0 collective-permute-done.3.where_ref
  23.2 0.0 copy-start.4
  23.2 0.6 copy-done.4
  23.8 10.8 %shard_map.142 = bf16[16,208,256]{2,1,0:T(8,128)(2,1)} custom-call(bf16[1024,256]{1,0:T(8,128)(2,1)} %collective-permute-done.surf_ref, bf16[4,256,256]{2,1,0:T(8,128)(2,1)} %dynamic-slice_bitcast_fusion.table_ref, s32[8,1024]{1,0:T(8,128)} %copy-done.4), custom_call_target="tpu_custom_call" | custom-call | flops 6000000000 | bytes 8388608 | tf_op jit(solution)/shard_map/pallas_call | solution.py:326
  34.6 0.0 copy-start.5
  34.6 0.0 collective-permute-done.4
  34.6 0.0 copy-start.3
  34.6 0.7 copy-done.3
  35.3 0.0 collective-permute-done.5
  35.3 7.9 %all-to-all-start = ((bf16[16,208,256]{2,1,0:T(8,128)(2,1)}), bf16[16,208,256]{2,1,0:T(8,128)(2,1)}, u32[]{:S(2)}, u32[]{:S(2)}) async-start(bf16[16,208,256]{2,1,0:T(8,128)(2,1)} %shard_map.142), calls=%async_computation | async-start | bytes 3407872 | tf_op jit(solution)/shard_map/all_to_all | solution.py:426
  43.3 0.1 pad_add_fusion.1
  43.3 0.0 copy-done.5
  43.3 37.8 %conditional.1 = (f32[1024,768]{1,0:T(8,128)}) conditional(s32[]{:T(128)} %convert_element_type.14, (s32[2]{0:T(128)S(1)}, bf16[32,32,768]{2,1,0:T(8,128)(2,1)S(1)}, bf16[32,16,768]{2,1,0:T(8,128)(2,1)S(1)}, bf16[4,48,768]{2,1,0:T(8,128)(2,1)}, bf16[4,48,768]{2,1,0:T(8,128)(2,1)}, /*index=5*/bf16[768,2304]{1,0:T(8,128)(2,1)}, ...), branch_computations={%region_0.1_spmd, %region_1.2_spmd} | conditional | flops 60000002048 | bytes 8388616 | solution.py:430
  43.5 37.5 %branch_0_fun.1 = f32[1024,768]{1,0:T(8,128)} custom-call(s32[2]{0:T(128)S(1)} %get-tuple-element.40.place_ref, bf16[32,32,768]{2,1,0:T(8,128)(2,1)S(1)} %get-tuple-element.41.own_ref, bf16[32,16,768]{2,1,0:T(8,128)(2,1)S(1)} %get-tuple-element.42.side_ref, bf16[4,48,768]{2,1,0:T(8,128)(2,1)} %get-tuple-element.43.top_ref, ...), custom_call_target="tpu_custom_call" | custom-call | flops 60000002048 | bytes 8388608 | tf_op jit(solution)/shard_map/cond/branch_0_fun/pallas_call | solution.py:326
  81.2 1.6 %all-to-all-done.got_ref = bf16[16,208,256]{2,1,0:T(8,128)(2,1)} async-done(((bf16[16,208,256]{2,1,0:T(8,128)(2,1)}), bf16[16,208,256]{2,1,0:T(8,128)(2,1)}, u32[]{:S(2)}, u32[]{:S(2)}) %all-to-all-start) | async-done | bytes 1703968 | tf_op jit(solution)/shard_map/all_to_all | solution.py:426
  82.8 7.9 %shard_map.143 = bf16[32,32,768]{2,1,0:T(8,128)(2,1)} custom-call(bf16[16,208,256]{2,1,0:T(8,128)(2,1)} %all-to-all-done.got_ref, f32[1024,768]{1,0:T(8,128)} %get-tuple-element.86.core_ref, bf16[256,768]{1,0:T(8,128)(2,1)} %bitcast.28, f32[32,32]{1,0:T(8,128)} %get-tuple-element.84.sea_ref), custom_call_target="tpu_custom_call" | custom-call | flops 6000000000 | bytes 8388608 | tf_op jit(solution)/shard_map/pallas_call | solution.py:326
  (5 shorter events, 0.1 us)
Async XLA Ops:
  0.0 7.7 %copy-start = (bf16[2,4,256,256]{3,2,1,0:T(8,128)(2,1)S(1)}, bf16[2,4,256,256]{3,2,1,0:T(8,128)(2,1)}, u32[]{:S(2)}) copy-start(bf16[2,4,256,256]{3,2,1,0:T(8,128)(2,1)} %param.26) | copy-start | bytes 3145732
  0.9 22.3 %collective-permute-start.3 = (s32[8,1024]{1,0:T(8,128)S(1)}, s32[8,1024]{1,0:T(8,128)S(1)}, u32[]{:S(2)}, u32[]{:S(2)}) collective-permute-start(s32[8,1024]{1,0:T(8,128)S(1)} %pad_add_fusion), channel_id=1, source_target_pairs={{0,16},{16,0},{1,17},{17,1},{2,18},{18,2},{3,19},{19,3},{4,20},{20... | collective-permute-start | bytes 98312 | tf_op jit(solution)/shard_map/ppermute | solution.py:416
  2.4 3.9 %copy-start.2 = (bf16[1,768,256]{2,1,0:T(8,128)(2,1)S(1)}, bf16[1,768,256]{2,1,0:T(8,128)(2,1)}, u32[]{:S(2)}) copy-start(bf16[1,768,256]{2,1,0:T(8,128)(2,1)} %param.24) | copy-start | bytes 1179652
  4.3 7.7 %collective-permute-start.1 = (bf16[32,4,768]{2,1,0:T(4,128)(2,1)S(1)}, bf16[32,4,768]{2,1,0:T(4,128)(2,1)S(1)}, u32[]{:S(2)}, u32[]{:S(2)}) collective-permute-start(bf16[32,4,768]{2,1,0:T(4,128)(2,1)S(1)} %get-tuple-element.80), channel_id=1, source_target_pairs={{1,0},{2,1},{3,2},{0,3},{5,4},{6,5},{7,6},{4,7},{9,8},{10,9},{11,1... | collective-permute-start | bytes 589832 | tf_op jit(solution)/shard_map/ppermute | solution.py:388
  5.8 10.1 %collective-permute-start.2 = (bf16[32,4,768]{2,1,0:T(4,128)(2,1)S(1)}, bf16[32,4,768]{2,1,0:T(4,128)(2,1)}, u32[]{:S(2)}, u32[]{:S(2)}) collective-permute-start(bf16[32,4,768]{2,1,0:T(4,128)(2,1)S(1)} %get-tuple-element.81), channel_id=1, source_target_pairs={{0,1},{1,2},{2,3},{3,0},{4,5},{5,6},{6,7},{7,4},{8,9},{9,10},{10,1... | collective-permute-start | bytes 589832 | tf_op jit(solution)/shard_map/ppermute | solution.py:388
  7.7 9.5 %collective-permute-start = (bf16[1024,256]{1,0:T(8,128)(2,1)}, bf16[1024,256]{1,0:T(8,128)(2,1)}, u32[]{:S(2)}, u32[]{:S(2)}) collective-permute-start(bf16[1024,256]{1,0:T(8,128)(2,1)} %convolution_convert_fusion), channel_id=1, source_target_pairs={{0,16},{16,0},{1,17},{17,1},{2,18},{18,2},{3,19},{19,3},{4,20},{20... | collective-permute-start | bytes 1572872 | tf_op jit(solution)/shard_map/ppermute | solution.py:419
  12.0 0.7 copy-start.1
  17.2 17.4 %collective-permute-start.4 = (bf16[4,48,768]{2,1,0:T(8,128)(2,1)S(1)}, bf16[4,48,768]{2,1,0:T(8,128)(2,1)S(1)}, u32[]{:S(2)}, u32[]{:S(2)}) collective-permute-start(bf16[4,48,768]{2,1,0:T(8,128)(2,1)S(1)} %pad_maximum_fusion.1), channel_id=1, source_target_pairs={{0,4},{4,8},{8,12},{1,5},{5,9},{9,13},{2,6},{6,10},{10,14},{3,7},{... | collective-permute-start | bytes 884744 | tf_op jit(solution)/shard_map/ppermute | solution.py:388
  20.8 14.6 %collective-permute-start.5 = (bf16[4,48,768]{2,1,0:T(8,128)(2,1)S(1)}, bf16[4,48,768]{2,1,0:T(8,128)(2,1)}, u32[]{:S(2)}, u32[]{:S(2)}) collective-permute-start(bf16[4,48,768]{2,1,0:T(8,128)(2,1)S(1)} %pad_maximum_fusion.2), channel_id=1, source_target_pairs={{4,0},{8,4},{12,8},{5,1},{9,5},{13,9},{6,2},{10,6},{14,10},{7,3},{... | collective-permute-start | bytes 884744 | tf_op jit(solution)/shard_map/ppermute | solution.py:388
  23.2 0.6 copy-start.4
  34.6 8.7 %copy-start.5 = (f32[4,128]{1,0:T(4,128)S(1)}, f32[4,128]{1,0:T(4,128)}, u32[]{:S(2)}) copy-start(f32[4,128]{1,0:T(4,128)} %param.23) | copy-start | bytes 6148
  34.6 0.7 copy-start.3
  35.3 47.5 %all-to-all-start = ((bf16[16,208,256]{2,1,0:T(8,128)(2,1)}), bf16[16,208,256]{2,1,0:T(8,128)(2,1)}, u32[]{:S(2)}, u32[]{:S(2)}) async-start(bf16[16,208,256]{2,1,0:T(8,128)(2,1)} %shard_map.142), calls=%async_computation | async-start | bytes 3407872 | tf_op jit(solution)/shard_map/all_to_all | solution.py:426
